TPU v7x, 32 devices: a whole 2x2x4 slice. The times are simulated.
32 devices in a mesh: node: 8 (over y, x, core), local: 4 (over z).
Axes of the slice: x: 2, y: 2, z: 4, core: 2. Of those that a mesh axis runs over, the one named last changes fastest.
Arguments:
- grad_out: bfloat16 [4096, 32, 384], P(('node', 'local')), may hold values from -6 to 6
- pooled: bfloat16 [4096, 32, 256], P(('node', 'local')), may hold values from -6 to 6
- proj: bfloat16 [32, 256, 128], P(('node', 'local')), may hold values from -0.5 to 0.5
- assign: int32 [32], replicated, may hold values from 0 to 31, each once
- indices: int32 [32, 4096, 3, 8], P(('node', 'local')), may hold values from 0 to 511
- lengths: int32 [32, 4096, 3], P(('node', 'local')), may hold values from 1 to 8
Outputs:
- table_grad: float32 [32, 512, 256], P(('node', 'local'))
- proj_grad: float32 [32, 256, 128], P(('node', 'local'))
Inputs may be any that keep to these rules, and one draw needn't show every extreme that they name: assign holds every group id once.
All inputs are finite; a program needn't handle non-finite values.
Results may differ from a plain program's by a relative error of at most 0.0029.
Values may be sent and summed in bfloat16 or wider, within the bound.
No kernel may reach another device: no remote copies, remote signals or barrier semaphores. Data moves between devices by JAX's collectives and lax.ppermute only.
A program may use at most 192 MiB of HBM per device.

v0:
```python
import functools
import math

import jax
import jax.numpy as jnp
from jax import lax
from jax.experimental import pallas as pl
from jax.experimental.pallas import tpu as pltpu
from jax.sharding import PartitionSpec as P

ROWS = 512
W1 = 16
W2 = 48
W3 = 192
PD = 128
W12 = W1 + W2
WSUM = W12 + W3
AXES = ("node", "local")
EB = 8
STEP = 32
MIB = 1024 * 1024


def params(grid):
    return pltpu.CompilerParams(dimension_semantics=("arbitrary",) * grid, vmem_limit_bytes=58 * MIB)


HBM = pl.BlockSpec(memory_space=pltpu.HBM)
ANY = pl.BlockSpec(memory_space=pl.ANY)


def cost(flops):
    return pl.CostEstimate(flops=int(flops), bytes_accessed=1024, transcendentals=0)


def permute_kernel(slots, pieces, assign_ref, grad_ref, pool_ref, *refs):
    outs, (perm_ref, grad_held, pool_held, sems) = refs[:3], refs[3:]
    step = pl.program_id(0)
    sources = ((grad_ref, grad_held), (pool_ref, pool_held))

    def copies(i):
        at = pl.ds(i * STEP, STEP)
        return [
            pltpu.make_async_copy(ref.at[at], held.at[at], sems.at[n, i]) for n, (ref, held) in enumerate(sources)
        ]

    @pl.when(step == 0)
    def _():
        for i in range(grad_ref.shape[0] // STEP):
            for copy in copies(i):
                copy.start()
        width = EB * slots
        lane = lax.broadcasted_iota(jnp.int32, (2 * EB, width), 1)
        row = lax.broadcasted_iota(jnp.int32, (2 * EB, width), 0)
        for s in range(0, slots, 2):
            group = jnp.where(row < EB, assign_ref[s], assign_ref[s + 1])
            hit = lane == (row % EB) * slots + group
            perm_ref[s * EB : (s + 2) * EB, :] = jnp.where(hit, 1.0, 0.0).astype(jnp.bfloat16)

    for copy, (_, held), cuts in zip(copies(step), sources, pieces):
        copy.wait()
        width = held.shape[2]
        for start in range(0, STEP, 2 * EB):
            pair = []
            for at in (start, start + EB):
                block = held[pl.ds(step * STEP + at, EB)].reshape(EB * slots, width)
                moved = jnp.dot(perm_ref[...], block, preferred_element_type=jnp.float32)
                pair.append(moved.reshape(slots, EB, width))
            both = jnp.concatenate(pair, axis=1).astype(jnp.bfloat16)
            for n, low, high in cuts:
                outs[n][:, start : start + 2 * EB, :] = both[:, :, low:high]


def permute(assign, grad_out, pooled):
    count, slots, _ = grad_out.shape
    widths = (2 * PD, PD, WSUM)
    pieces = (((0, 0, 2 * PD), (1, 2 * PD, 3 * PD)), ((2, 0, WSUM),))
    return pl.pallas_call(
        functools.partial(permute_kernel, slots, pieces),
        out_shape=[jax.ShapeDtypeStruct((slots, count, width), jnp.bfloat16) for width in widths],
        grid_spec=pltpu.PrefetchScalarGridSpec(
            num_scalar_prefetch=1,
            grid=(count // STEP,),
            in_specs=[HBM] * 2,
            out_specs=[pl.BlockSpec((slots, STEP, width), lambda i, a: (0, i, 0)) for width in widths],
            scratch_shapes=[
                pltpu.VMEM((EB * slots, EB * slots), jnp.bfloat16),
                pltpu.VMEM(grad_out.shape, jnp.bfloat16),
                pltpu.VMEM(pooled.shape, jnp.bfloat16),
                pltpu.SemaphoreType.DMA((2, count // STEP)),
            ],
        ),
        compiler_params=params(1),
        cost_estimate=cost(1e7),
        name="permute_groups",
    )(assign, grad_out, pooled)


def fetch(ref, held, sems, blocks, pick=lambda i: i):
    size = held.shape[0] // blocks
    copies = [
        pltpu.make_async_copy(ref.at[pl.ds(pick(i) * size, size)], held.at[pl.ds(i * size, size)], sems.at[i])
        for i in range(blocks)
    ]
    for copy in copies:
        copy.start()
    return copies


def narrow_kernel(blocks, place_ref, g_ref, w_ref, *refs):
    out_ref, g_held, w_held, out_held, g_sems, w_sems, out_sems = refs[-7:]
    weights = fetch(w_ref, w_held, w_sems, 1)
    loads = fetch(g_ref, g_held, g_sems, blocks)
    slots, count, _ = g_held.shape
    step, half = slots // blocks, count // 2
    column = lax.broadcasted_iota(jnp.int32, (count, W12), 1)
    dims = (((1,), (1,)), ((), ()))
    weights[0].wait()
    stores = []
    for i, load in enumerate(loads):
        load.wait()
        for s in range(i * step, (i + 1) * step):
            w = w_held[place_ref[s]]
            first = lax.dot_general(g_held[s, :, :PD], w, dims, preferred_element_type=jnp.float32)
            second = lax.dot_general(g_held[s, :, PD:], w, dims, preferred_element_type=jnp.float32)
            d = jnp.where(column < W1, first, second)
            out_held[s] = jnp.concatenate([d[:half], d[half:]], axis=1).astype(jnp.bfloat16)
        at = pl.ds(i * step, step)
        stores.append(pltpu.make_async_copy(out_held.at[at], out_ref.at[at], out_sems.at[i]))
        stores[-1].start()
    for store in stores:
        store.wait()


def narrow_dpool(place, g12, w12, after=()):
    slots, count, _ = g12.shape
    blocks = 4
    shape = (slots, count // 2, 2 * W12)
    return pl.pallas_call(
        functools.partial(narrow_kernel, blocks),
        out_shape=jax.ShapeDtypeStruct(shape, jnp.bfloat16),
        grid_spec=pltpu.PrefetchScalarGridSpec(
            num_scalar_prefetch=1,
            grid=(1,),
            in_specs=[HBM] * 2 + [ANY] * len(after),
            out_specs=HBM,
            scratch_shapes=[
                pltpu.VMEM(g12.shape, jnp.bfloat16),
                pltpu.VMEM(w12.shape, jnp.bfloat16),
                pltpu.VMEM(shape, jnp.bfloat16),
                pltpu.SemaphoreType.DMA((blocks,)),
                pltpu.SemaphoreType.DMA((1,)),
                pltpu.SemaphoreType.DMA((blocks,)),
            ],
        ),
        compiler_params=params(1),
        cost_estimate=cost(1e7),
        name="narrow_dpool",
    )(place, g12, w12, *after)


def partial_kernel(ins, added, results, node_ref, line_ref, *refs):
    blocks, size = node_ref.shape[0], line_ref.shape[0]
    operands, others = refs[:ins], refs[ins : ins + added]
    outs, scratch = refs[-3 - 2 * results - ins - added :][:results], refs[-3 - results - ins - added :]
    held, other_held, out_held = scratch[:ins], scratch[ins : ins + added], scratch[ins + added : -3]
    in_sems, other_sems, out_sems = scratch[-3:]

    def block(arrays, i):
        per = blocks // len(arrays)
        return arrays[i // per].at[pl.ds(i % per * size, size)]

    loads = [
        fetch(ref, at, in_sems.at[n], blocks, lambda i: node_ref[i])
        for n, (ref, at) in enumerate(zip(operands, held))
    ]
    if added:
        loads.append(
            [
                pltpu.make_async_copy(block(others, i), block(other_held, i), other_sems.at[i])
                for i in range(blocks)
            ]
        )
        for copy in loads[-1]:
            copy.start()
    stores = []
    for i in range(blocks):
        for copies in loads:
            copies[i].wait()
        out = block(out_held, i)
        for l in range(size):
            slot = i * size + line_ref[l]
            q = held[0][slot].T
            narrow = jnp.dot(q[:W12], held[1][slot], preferred_element_type=jnp.float32)
            wide = jnp.dot(q[W12:], held[2][slot], preferred_element_type=jnp.float32)
            pieces = ((0, W1, narrow[:W1, :PD]), (W1, W12, narrow[W1:, PD:]), (W12, WSUM, wide))
            for start, end, piece in pieces:
                if added:
                    piece = piece + block(other_held, i)[l, start:end]
                out[l, start:end] = piece.astype(out.dtype)
        stores.append(pltpu.make_async_copy(out, block(outs, i), out_sems.at[i]))
        stores[-1].start()
    for store in stores:
        store.wait()


def partial_proj(nodes, lines, q, g12, g3, results, others=(), after=()):
    _, count, _ = q.shape
    blocks, size = nodes.shape[0], lines.shape[0]
    kinds = [jnp.bfloat16 if others and i else jnp.float32 for i in range(results)]
    shapes = [jax.ShapeDtypeStruct((blocks // results * size, WSUM, PD), kind) for kind in kinds]
    operands = (q, g12, g3)
    return pl.pallas_call(
        functools.partial(partial_kernel, len(operands), len(others), results),
        out_shape=shapes,
        grid_spec=pltpu.PrefetchScalarGridSpec(
            num_scalar_prefetch=2,
            grid=(1,),
            in_specs=[HBM] * (len(operands) + len(others)) + [ANY] * len(after),
            out_specs=[HBM] * results,
            scratch_shapes=[pltpu.VMEM((blocks * size, count, x.shape[2]), jnp.bfloat16) for x in operands]
            + [pltpu.VMEM(x.shape, x.dtype) for x in others]
            + [pltpu.VMEM(x.shape, x.dtype) for x in shapes]
            + [
                pltpu.SemaphoreType.DMA((len(operands), blocks)),
                pltpu.SemaphoreType.DMA((blocks,)),
                pltpu.SemaphoreType.DMA((blocks,)),
            ],
        ),
        compiler_params=params(1),
        cost_estimate=cost(1e7),
        name="partial_proj",
    )(nodes, lines, *operands, *others, *after)


def count_kernel(index_ref, length_ref, *refs):
    out_ref = refs[-1]
    bag, block = index_ref.shape[1], index_ref.shape[2]
    lanes, chunk, low = 256, 16, ROWS // 8

    def one(i, carry):
        at = pl.ds(pl.multiple_of(i * lanes, lanes), lanes)
        index = index_ref[0, :, at]
        which = lax.broadcasted_iota(jnp.int32, (bag, lanes), 0)
        key = jnp.where(which < length_ref[0, :, at], index & (low - 1), -1)
        unit = jnp.left_shift(jnp.int32(1), jnp.right_shift(index, 6) * 4)
        ids = lax.broadcasted_iota(jnp.int32, (chunk, lanes), 0)
        for c in range(low // chunk):
            total = jnp.zeros((chunk, lanes), jnp.int32)
            for j in range(bag):
                total = total + jnp.where(key[j : j + 1] == ids + c * chunk, unit[j : j + 1], 0)
            out_ref[0, c * chunk : (c + 1) * chunk, at] = total
        return carry

    lax.fori_loop(0, block // lanes, one, 0)


def count_hits(lookups, counts, after=()):
    tables, bag, examples = lookups.shape
    block = 4096
    return pl.pallas_call(
        count_kernel,
        out_shape=jax.ShapeDtypeStruct((tables, ROWS // 8, examples), jnp.int32),
        grid=(tables, examples // block),
        in_specs=[
            pl.BlockSpec((1, bag, block), lambda k, i: (k, 0, i)),
            pl.BlockSpec((1, 1, block), lambda k, i: (k, 0, i)),
        ]
        + [ANY] * len(after),
        out_specs=pl.BlockSpec((1, ROWS // 8, block), lambda k, i: (k, 0, i)),
        compiler_params=params(2),
        cost_estimate=cost(1e7),
        name="count_hits",
    )(lookups, counts, *after)


def unpacked(words):
    rows = [lax.shift_right_logical(words, jnp.int32(4 * n)) & 15 for n in range(8)]
    return jnp.concatenate([r.astype(jnp.float32).astype(jnp.bfloat16) for r in rows], axis=0)


def wide_kernel(hits_ref, g_ref, w_ref, *refs):
    out_ref = refs[-1]

    @pl.when(pl.program_id(0) == 0)
    def _():
        out_ref[...] = jnp.zeros_like(out_ref)

    block = g_ref.shape[0]
    column = lax.broadcasted_iota(jnp.int32, (block, WSUM), 1)
    d = lax.dot_general(g_ref[...], w_ref[...], (((1,), (1,)), ((), ())), preferred_element_type=jnp.float32)
    d = jnp.where(column < W12, 0.0, d).astype(jnp.bfloat16)
    out_ref[...] += jnp.dot(unpacked(hits_ref[0]), d, preferred_element_type=jnp.float32)


def wide_sum(hits, g3, weights, after=()):
    _, words, examples = hits.shape
    block = 1024
    return pl.pallas_call(
        wide_kernel,
        out_shape=jax.ShapeDtypeStruct((ROWS, WSUM), jnp.float32),
        grid=(examples // block,),
        in_specs=[
            pl.BlockSpec((1, words, block), lambda i: (2, 0, i)),
            pl.BlockSpec((block, PD), lambda i: (i, 0)),
            pl.BlockSpec((WSUM, PD), lambda i: (0, 0)),
        ]
        + [ANY] * len(after),
        out_specs=pl.BlockSpec((ROWS, WSUM), lambda i: (0, 0)),
        compiler_params=params(1),
        cost_estimate=cost(1e7),
        name="wide_sum",
    )(hits, g3, weights, *after)


def narrow_sum_kernel(hits_ref, d_ref, wide_ref, *refs):
    out_ref = refs[-1]

    @pl.when(pl.program_id(0) == 0)
    def _():
        out_ref[...] = wide_ref[...]

    sources = d_ref.shape[0]
    block = hits_ref.shape[2]
    column = lax.broadcasted_iota(jnp.int32, (block, PD), 1)
    pieces = []
    for d in range(sources):
        packed = d_ref[d].astype(jnp.float32)
        pieces += [packed, pltpu.roll(packed, PD - W12, 1)]
    both = jnp.concatenate(pieces, axis=0)
    d1 = jnp.where(column < W1, both, 0.0).astype(jnp.bfloat16)
    d2 = jnp.where((column >= W1) & (column < W12), both, 0.0).astype(jnp.bfloat16)
    out_ref[...] += jnp.dot(unpacked(hits_ref[0]), d1, preferred_element_type=jnp.float32) + jnp.dot(
        unpacked(hits_ref[1]), d2, preferred_element_type=jnp.float32
    )


def narrow_sum(hits, narrow, wide, after=()):
    _, words, examples = hits.shape
    sources, half, _ = narrow.shape
    block = 1024
    per = block // (2 * half)
    return pl.pallas_call(
        narrow_sum_kernel,
        out_shape=jax.ShapeDtypeStruct((ROWS, WSUM), jnp.float32),
        grid=(examples // block,),
        in_specs=[
            pl.BlockSpec((2, words, block), lambda i: (0, 0, i)),
            pl.BlockSpec((per, half, 2 * W12), lambda i: (i, 0, 0)),
            pl.BlockSpec((ROWS, PD), lambda i: (0, 0)),
        ]
        + [ANY] * len(after),
        out_specs=pl.BlockSpec((ROWS, PD), lambda i: (0, 0)),
        input_output_aliases={2: 0},
        compiler_params=params(1),
        cost_estimate=cost(1e7),
        name="narrow_sum",
    )(hits, narrow, wide, *after)


def swap(x, axis, size, bits):
    return lax.ppermute(x, axis, [(d, d ^ bits) for d in range(size)])


def local(sizes, grad_out, pooled, proj, assign, indices, lengths):
    count, slots, _ = grad_out.shape
    scale = 1.0 / math.sqrt(count * slots)
    n_node, n_local = sizes["node"], sizes["local"]
    n_plane = n_node // 2
    node, loc = lax.axis_index("node"), lax.axis_index("local")

    rows = proj[:, :W12]
    rows = jnp.concatenate([rows] + [swap(rows, "local", n_local, d) for d in range(1, n_local)])
    g12, g3, q = permute(assign, grad_out, pooled)
    rows, g3 = lax.optimization_barrier((rows, g3))
    g3_got = lax.all_to_all(g3, AXES, split_axis=0, concat_axis=0, tiled=True)

    plane = jnp.arange(n_plane, dtype=jnp.int32) ^ (node // 2)
    lines = jnp.arange(n_local, dtype=jnp.int32) ^ loc
    sent = partial_proj(plane * 2 + 1 - node % 2, lines, q, g12, g3, 2)
    got = [swap(x, "node", n_node, 1) for x in sent]

    rows, sent = lax.optimization_barrier((rows, sent))
    rows = jnp.concatenate([rows] + [swap(rows, "node", n_node, 2 * d) for d in range(1, n_plane)])
    hits = count_hits(indices[0].transpose(1, 2, 0), lengths[0].T[:, None, :], after=sent[:1])
    kept = partial_proj(plane * 2 + node % 2, lines, q, g12, g3, n_plane, got, after=[rows, hits])
    arrived = [swap(kept[d], "node", n_node, 2 * d) for d in range(1, n_plane)]

    rows = jnp.concatenate([rows, swap(rows, "node", n_node, 1)])
    slot = jnp.arange(slots, dtype=jnp.int32)
    slot_node = slot // n_local ^ node
    slot_place = slot_node % 2 * (slots // 2) + slot_node // 2 * n_local + (slot % n_local ^ loc)
    narrow = narrow_dpool(slot_place, g12, rows, after=kept[:1])
    narrow, g3_got, arrived = lax.optimization_barrier((narrow, g3_got, arrived))
    narrow_got = lax.all_to_all(narrow, AXES, split_axis=0, concat_axis=0, tiled=True)
    total = kept[0]
    for term in arrived:
        total = total + term.astype(jnp.float32)
    wide = wide_sum(hits, g3_got.reshape(-1, PD), proj[0])
    total, wide = lax.optimization_barrier((total, wide))
    rounded = total.astype(jnp.bfloat16)
    own, terms = total[:1], [swap(rounded[d : d + 1], "local", n_local, d) for d in range(1, n_local)]

    table_grad = narrow_sum(hits, narrow_got, wide)[None]
    terms, table_grad = lax.optimization_barrier((terms, table_grad))
    proj_grad = sum((term.astype(jnp.float32) for term in terms), own) * scale
    return (table_grad, proj_grad)


def solution(mesh):
    placed = (
        P(AXES, None, None),
        P(AXES, None, None),
        P(AXES, None, None),
        P(),
        P(AXES, None, None, None),
        P(AXES, None, None),
    )
    return jax.shard_map(
        functools.partial(local, dict(mesh.shape)),
        mesh=mesh,
        in_specs=placed,
        out_specs=(P(AXES, None, None), P(AXES, None, None)),
        check_vma=False,
    )
```

profile of v0, /device:TPU:1, one launch (start us, length us, event | category | flops | bytes accessed | tf_op | source)
XLA Modules:
  0.0 93.6 jit_solution(12518073892485550065)
XLA Ops:
  1.4 4.2 %collective-permute-start.2 = (bf16[1,64,128]{2,1,0:T(8,128)(2,1)S(1)}, bf16[1,64,128]{2,1,0:T(8,128)(2,1)S(1)}, u32[]{:S(2)}, u32[]{:S(2)}) collective-permute-start(bf16[1,64,128]{2,1,0:T(8,128)(2,1)S(1)} %slice.15), channel_id=1, source_target_pairs={{0,3},{1,2},{2,1},{3,0},{4,7},{5,6},{6,5},{7,4},{8,11},{9,10},{10,... | collective-permute-start | bytes 49160 | tf_op jit(solution)/shard_map/ppermute | solution.py:362
  5.8 6.5 %permute_groups.1 = (bf16[32,128,256]{2,1,0:T(8,128)(2,1)}, bf16[32,128,128]{2,1,0:T(8,128)(2,1)}, bf16[32,128,256]{2,1,0:T(8,128)(2,1)}) custom-call(s32[32]{0:T(128)} %assign_ref.1, bf16[128,32,384]{2,1,0:T(8,128)(2,1)} %grad_ref.1, bf16[128,32,256]{2,1,0:T(8,128)(2,1)} %pool_ref.1), custom_call_target="tpu_custom_call" | custom-call | flops 10000000 | bytes 1024 | tf_op jit(solution)/shard_map/permute_groups/pallas_call | solution.py:78
  12.3 7.1 %all-to-all-start = ((bf16[32,128,128]{2,1,0:T(8,128)(2,1)}), bf16[32,128,128]{2,1,0:T(8,128)(2,1)S(1)}, u32[]{:S(2)}, u32[]{:S(2)}) async-start(bf16[32,128,128]{2,1,0:T(8,128)(2,1)} %get-tuple-element.29.refs_2_), calls=%async_computation | async-start | bytes 2097152 | tf_op jit(solution)/shard_map/all_to_all | solution.py:376
  20.0 4.5 %partial_proj.2 = (f32[8,256,128]{2,1,0:T(8,128)}, f32[8,256,128]{2,1,0:T(8,128)}) custom-call(s32[4]{0:T(128)} %get-tuple-element.61.node_ref, s32[4]{0:T(128)} %get-tuple-element.62.line_ref, bf16[32,128,256]{2,1,0:T(8,128)(2,1)} %get-tuple-element.26.refs_0_, bf16[32,128,256]{2,1,0:T(8,128)(2,1)} %get-tuple-element.27.refs_1_.g_ref, ...), custom_call_target="tpu_custom_call" | custom-call | flops 10000000 | bytes 1024 | tf_op jit(solution)/shard_map/partial_proj/pallas_call | solution.py:213
  25.0 1.4 %collective-permute-start.5 = (bf16[4,64,128]{2,1,0:T(8,128)(2,1)S(1)}, bf16[4,64,128]{2,1,0:T(8,128)(2,1)S(1)}, u32[]{:S(2)}, u32[]{:S(2)}) collective-permute-start(bf16[4,64,128]{2,1,0:T(8,128)(2,1)S(1)} %pad_maximum_fusion), channel_id=1, source_target_pairs={{0,8},{4,12},{8,0},{12,4},{16,24},{20,28},{24,16},{28,20},{1,9},{5... | collective-permute-start | bytes 196616 | tf_op jit(solution)/shard_map/ppermute | solution.py:362
  26.4 1.2 %collective-permute-start.6 = (bf16[4,64,128]{2,1,0:T(8,128)(2,1)S(1)}, bf16[4,64,128]{2,1,0:T(8,128)(2,1)S(1)}, u32[]{:S(2)}, u32[]{:S(2)}) collective-permute-start(bf16[4,64,128]{2,1,0:T(8,128)(2,1)S(1)} %pad_maximum_fusion), channel_id=1, source_target_pairs={{0,16},{4,20},{8,24},{12,28},{16,0},{20,4},{24,8},{28,12},{1,17},{... | collective-permute-start | bytes 196616 | tf_op jit(solution)/shard_map/ppermute | solution.py:362
  27.7 1.8 %collective-permute-done.5 = bf16[4,64,128]{2,1,0:T(8,128)(2,1)S(1)} collective-permute-done((bf16[4,64,128]{2,1,0:T(8,128)(2,1)S(1)}, bf16[4,64,128]{2,1,0:T(8,128)(2,1)S(1)}, u32[]{:S(2)}, u32[]{:S(2)}) %collective-permute-start.5) | collective-permute-done | bytes 65568 | tf_op jit(solution)/shard_map/ppermute | solution.py:362
  29.5 1.6 %collective-permute-done.6 = bf16[4,64,128]{2,1,0:T(8,128)(2,1)S(1)} collective-permute-done((bf16[4,64,128]{2,1,0:T(8,128)(2,1)S(1)}, bf16[4,64,128]{2,1,0:T(8,128)(2,1)S(1)}, u32[]{:S(2)}, u32[]{:S(2)}) %collective-permute-start.6) | collective-permute-done | bytes 65568 | tf_op jit(solution)/shard_map/ppermute | solution.py:362
  31.1 2.5 %collective-permute-done.7 = bf16[4,64,128]{2,1,0:T(8,128)(2,1)S(1)} collective-permute-done((bf16[4,64,128]{2,1,0:T(8,128)(2,1)S(1)}, bf16[4,64,128]{2,1,0:T(8,128)(2,1)S(1)}, u32[]{:S(2)}, u32[]{:S(2)}) %collective-permute-start.7) | collective-permute-done | bytes 65568 | tf_op jit(solution)/shard_map/ppermute | solution.py:362
  35.7 4.9 %count_hits.1.refs_6_.hits_ref = s32[3,64,4096]{2,1,0:T(8,128)} custom-call(s32[3,8,4096]{2,1,0:T(8,128)} %bitcast.13, s32[3,1,4096]{2,1,0:T(1,128)} %broadcast_in_dim.6.length_ref, f32[8,256,128]{2,1,0:T(8,128)} %get-tuple-element.34.refs_0_), custom_call_target="tpu_custom_call" | custom-call | flops 10000000 | bytes 1024 | tf_op jit(solution)/shard_map/count_hits/pallas_call | solution.py:261
  40.7 1.0 %copy-done.3 = f32[8,256,128]{2,1,0:T(8,128)} copy-done((f32[8,256,128]{2,1,0:T(8,128)}, f32[8,256,128]{2,1,0:T(8,128)S(1)}, u32[]{:S(2)}) %copy-start.3) | copy-done | bytes 1048600
  41.7 1.0 %copy-done.4 = f32[8,256,128]{2,1,0:T(8,128)} copy-done((f32[8,256,128]{2,1,0:T(8,128)}, f32[8,256,128]{2,1,0:T(8,128)S(1)}, u32[]{:S(2)}) %copy-start.4) | copy-done | bytes 1048600
  42.7 4.4 %partial_proj.3 = (f32[4,256,128]{2,1,0:T(8,128)}, bf16[4,256,128]{2,1,0:T(8,128)(2,1)}, bf16[4,256,128]{2,1,0:T(8,128)(2,1)}, bf16[4,256,128]{2,1,0:T(8,128)(2,1)}) custom-call(s32[4]{0:T(128)} %fusion.5.node_ref, s32[4]{0:T(128)} %get-tuple-element.62.line_ref, bf16[32,128,256]{2,1,0:T(8,128)(2,1)} %get-tuple-element.26.refs_0_, ...), custom_call_target="tpu_custom_call" | custom-call | flops 10000000 | bytes 1024 | tf_op jit(solution)/shard_map/partial_proj/pallas_call | solution.py:213
  47.1 1.3 %collective-permute-start.9 = (bf16[4,256,128]{2,1,0:T(8,128)(2,1)}, bf16[4,256,128]{2,1,0:T(8,128)(2,1)S(1)}, u32[]{:S(2)}, u32[]{:S(2)}) collective-permute-start(bf16[4,256,128]{2,1,0:T(8,128)(2,1)} %get-tuple-element.36), channel_id=1, source_target_pairs={{0,8},{4,12},{8,0},{12,4},{16,24},{20,28},{24,16},{28,20},{1,9},{5... | collective-permute-start | bytes 786440 | tf_op jit(solution)/shard_map/ppermute | solution.py:362
  48.4 0.9 collective-permute-start.10
  51.2 4.4 %narrow_dpool.1 = bf16[32,64,128]{2,1,0:T(8,128)(2,1)} custom-call(s32[32]{0:T(128)} %fusion.1.place_ref, bf16[32,128,256]{2,1,0:T(8,128)(2,1)} %get-tuple-element.27.refs_1_.g_ref, bf16[32,64,128]{2,1,0:T(8,128)(2,1)} %copy-done.5, f32[4,256,128]{2,1,0:T(8,128)} %get-tuple-element.35.refs_0_), custom_call_target="tpu_custom_call" | custom-call | flops 10000000 | bytes 1024 | tf_op jit(solution)/shard_map/narrow_dpool/pallas_call | solution.py:139
  55.5 1.0 %collective-permute-done.10 = bf16[4,256,128]{2,1,0:T(8,128)(2,1)S(1)} collective-permute-done((bf16[4,256,128]{2,1,0:T(8,128)(2,1)}, bf16[4,256,128]{2,1,0:T(8,128)(2,1)S(1)}, u32[]{:S(2)}, u32[]{:S(2)}) %collective-permute-start.10) | collective-permute-done | bytes 262176 | tf_op jit(solution)/shard_map/ppermute | solution.py:362
  56.6 4.8 %collective-permute-done.11 = bf16[4,256,128]{2,1,0:T(8,128)(2,1)S(1)} collective-permute-done((bf16[4,256,128]{2,1,0:T(8,128)(2,1)}, bf16[4,256,128]{2,1,0:T(8,128)(2,1)S(1)}, u32[]{:S(2)}, u32[]{:S(2)}) %collective-permute-start.11) | collective-permute-done | bytes 262176 | tf_op jit(solution)/shard_map/ppermute | solution.py:362
  61.4 6.9 %all-to-all-start.1 = ((bf16[32,64,128]{2,1,0:T(8,128)(2,1)}), bf16[32,64,128]{2,1,0:T(8,128)(2,1)S(1)}, u32[]{:S(2)}, u32[]{:S(2)}) async-start(bf16[32,64,128]{2,1,0:T(8,128)(2,1)} %narrow_dpool.1), calls=%async_computation.1 | async-start | bytes 1048576 | tf_op jit(solution)/shard_map/all_to_all | solution.py:395
  68.3 5.5 %wide_sum.1.wide_ref = f32[512,256]{1,0:T(8,128)} custom-call(s32[3,64,4096]{2,1,0:T(8,128)} %count_hits.1.refs_6_.hits_ref, bf16[4096,128]{1,0:T(8,128)(2,1)} %bitcast.11, bf16[256,128]{1,0:T(8,128)(2,1)} %bitcast.15), custom_call_target="tpu_custom_call" | custom-call | flops 10000000 | bytes 1024 | tf_op jit(solution)/shard_map/wide_sum/pallas_call | solution.py:299
  74.0 1.5 %collective-permute-start.12 = (bf16[1,256,128]{2,1,0:T(8,128)(2,1)S(1)}, bf16[1,256,128]{2,1,0:T(8,128)(2,1)S(1)}, u32[]{:S(2)}, u32[]{:S(2)}) collective-permute-start(bf16[1,256,128]{2,1,0:T(8,128)(2,1)S(1)} %get-tuple-element.52), channel_id=1, source_target_pairs={{0,1},{1,0},{2,3},{3,2},{4,5},{5,4},{6,7},{7,6},{8,9},{9,8},{10,11... | collective-permute-start | bytes 196616 | tf_op jit(solution)/shard_map/ppermute | solution.py:362
  75.4 2.1 %collective-permute-start.13 = (bf16[1,256,128]{2,1,0:T(8,128)(2,1)S(1)}, bf16[1,256,128]{2,1,0:T(8,128)(2,1)S(1)}, u32[]{:S(2)}, u32[]{:S(2)}) collective-permute-start(bf16[1,256,128]{2,1,0:T(8,128)(2,1)S(1)} %get-tuple-element.51), channel_id=1, source_target_pairs={{0,2},{1,3},{2,0},{3,1},{4,6},{5,7},{6,4},{7,5},{8,10},{9,11},{10,... | collective-permute-start | bytes 196616 | tf_op jit(solution)/shard_map/ppermute | solution.py:362
  77.6 9.1 %all-to-all-done.1.d_ref = bf16[32,64,128]{2,1,0:T(8,128)(2,1)S(1)} async-done(((bf16[32,64,128]{2,1,0:T(8,128)(2,1)}), bf16[32,64,128]{2,1,0:T(8,128)(2,1)S(1)}, u32[]{:S(2)}, u32[]{:S(2)}) %all-to-all-start.1) | async-done | bytes 524320 | tf_op jit(solution)/shard_map/all_to_all | solution.py:395
  87.5 5.4 %narrow_sum.1 = f32[512,256]{1,0:T(8,128)} custom-call(s32[3,64,4096]{2,1,0:T(8,128)} %count_hits.1.refs_6_.hits_ref, bf16[32,64,128]{2,1,0:T(8,128)(2,1)} %copy-done.1, f32[512,256]{1,0:T(8,128)} %wide_sum.1.wide_ref), custom_call_target="tpu_custom_call", output_to_operand_aliasing={{}: (2, {})} | custom-call | flops 10000000 | bytes 1024 | tf_op jit(solution)/shard_map/narrow_sum/pallas_call | solution.py:343
  (49 shorter events, 7.9 us)
Async XLA Ops:
  1.4 10.9 %collective-permute-start.2 = (bf16[1,64,128]{2,1,0:T(8,128)(2,1)S(1)}, bf16[1,64,128]{2,1,0:T(8,128)(2,1)S(1)}, u32[]{:S(2)}, u32[]{:S(2)}) collective-permute-start(bf16[1,64,128]{2,1,0:T(8,128)(2,1)S(1)} %slice.15), channel_id=1, source_target_pairs={{0,3},{1,2},{2,1},{3,0},{4,7},{5,6},{6,5},{7,4},{8,11},{9,10},{10,... | collective-permute-start | bytes 49160 | tf_op jit(solution)/shard_map/ppermute | solution.py:362
  5.5 6.8 %collective-permute-start.1 = (bf16[1,64,128]{2,1,0:T(8,128)(2,1)S(1)}, bf16[1,64,128]{2,1,0:T(8,128)(2,1)S(1)}, u32[]{:S(2)}, u32[]{:S(2)}) collective-permute-start(bf16[1,64,128]{2,1,0:T(8,128)(2,1)S(1)} %slice.15), channel_id=1, source_target_pairs={{0,2},{1,3},{2,0},{3,1},{4,6},{5,7},{6,4},{7,5},{8,10},{9,11},{10,... | collective-permute-start | bytes 49160 | tf_op jit(solution)/shard_map/ppermute | solution.py:362
  5.5 6.8 %collective-permute-start = (bf16[1,64,128]{2,1,0:T(8,128)(2,1)S(1)}, bf16[1,64,128]{2,1,0:T(8,128)(2,1)S(1)}, u32[]{:S(2)}, u32[]{:S(2)}) collective-permute-start(bf16[1,64,128]{2,1,0:T(8,128)(2,1)S(1)} %slice.15), channel_id=1, source_target_pairs={{0,1},{1,0},{2,3},{3,2},{4,5},{5,4},{6,7},{7,6},{8,9},{9,8},{10,11... | collective-permute-start | bytes 49160 | tf_op jit(solution)/shard_map/ppermute | solution.py:362
  12.3 49.1 %all-to-all-start = ((bf16[32,128,128]{2,1,0:T(8,128)(2,1)}), bf16[32,128,128]{2,1,0:T(8,128)(2,1)S(1)}, u32[]{:S(2)}, u32[]{:S(2)}) async-start(bf16[32,128,128]{2,1,0:T(8,128)(2,1)} %get-tuple-element.29.refs_2_), calls=%async_computation | async-start | bytes 2097152 | tf_op jit(solution)/shard_map/all_to_all | solution.py:376
  20.0 14.5 %copy-start.7 = (s32[1,4096,3]{1,0,2:T(1,128)S(1)}, s32[1,4096,3]{1,0,2:T(1,128)}, u32[]{:S(2)}) copy-start(s32[1,4096,3]{1,0,2:T(1,128)} %param.11) | copy-start | bytes 147460
  24.4 16.2 %collective-permute-start.3 = (f32[8,256,128]{2,1,0:T(8,128)}, f32[8,256,128]{2,1,0:T(8,128)S(1)}, u32[]{:S(2)}, u32[]{:S(2)}) collective-permute-start(f32[8,256,128]{2,1,0:T(8,128)} %get-tuple-element.34.refs_0_), channel_id=1, source_target_pairs={{0,4},{4,0},{8,12},{12,8},{16,20},{20,16},{24,28},{28,24},{1,5},{5... | collective-permute-start | bytes 3145736 | tf_op jit(solution)/shard_map/ppermute | solution.py:362
  24.8 15.9 %collective-permute-start.4 = (f32[8,256,128]{2,1,0:T(8,128)}, f32[8,256,128]{2,1,0:T(8,128)S(1)}, u32[]{:S(2)}, u32[]{:S(2)}) collective-permute-start(f32[8,256,128]{2,1,0:T(8,128)} %get-tuple-element.31), channel_id=1, source_target_pairs={{0,4},{4,0},{8,12},{12,8},{16,20},{20,16},{24,28},{28,24},{1,5},{5... | collective-permute-start | bytes 3145736 | tf_op jit(solution)/shard_map/ppermute | solution.py:362
  25.0 4.5 %collective-permute-start.5 = (bf16[4,64,128]{2,1,0:T(8,128)(2,1)S(1)}, bf16[4,64,128]{2,1,0:T(8,128)(2,1)S(1)}, u32[]{:S(2)}, u32[]{:S(2)}) collective-permute-start(bf16[4,64,128]{2,1,0:T(8,128)(2,1)S(1)} %pad_maximum_fusion), channel_id=1, source_target_pairs={{0,8},{4,12},{8,0},{12,4},{16,24},{20,28},{24,16},{28,20},{1,9},{5... | collective-permute-start | bytes 196616 | tf_op jit(solution)/shard_map/ppermute | solution.py:362
  26.4 4.7 %collective-permute-start.6 = (bf16[4,64,128]{2,1,0:T(8,128)(2,1)S(1)}, bf16[4,64,128]{2,1,0:T(8,128)(2,1)S(1)}, u32[]{:S(2)}, u32[]{:S(2)}) collective-permute-start(bf16[4,64,128]{2,1,0:T(8,128)(2,1)S(1)} %pad_maximum_fusion), channel_id=1, source_target_pairs={{0,16},{4,20},{8,24},{12,28},{16,0},{20,4},{24,8},{28,12},{1,17},{... | collective-permute-start | bytes 196616 | tf_op jit(solution)/shard_map/ppermute | solution.py:362
  27.6 6.1 %collective-permute-start.7 = (bf16[4,64,128]{2,1,0:T(8,128)(2,1)S(1)}, bf16[4,64,128]{2,1,0:T(8,128)(2,1)S(1)}, u32[]{:S(2)}, u32[]{:S(2)}) collective-permute-start(bf16[4,64,128]{2,1,0:T(8,128)(2,1)S(1)} %pad_maximum_fusion), channel_id=1, source_target_pairs={{0,24},{4,28},{8,16},{12,20},{16,8},{20,12},{24,0},{28,4},{1,25},{... | collective-permute-start | bytes 196616 | tf_op jit(solution)/shard_map/ppermute | solution.py:362
  33.7 6.9 %copy-start.6 = (bf16[16,64,128]{2,1,0:T(8,128)(2,1)}, bf16[16,64,128]{2,1,0:T(8,128)(2,1)S(1)}, u32[]{:S(2)}) copy-start(bf16[16,64,128]{2,1,0:T(8,128)(2,1)S(1)} %get-tuple-element.53.refs_5_) | copy-start | bytes 786436
  33.7 16.6 %collective-permute-start.8 = (bf16[16,64,128]{2,1,0:T(8,128)(2,1)S(1)}, bf16[16,64,128]{2,1,0:T(8,128)(2,1)S(1)}, u32[]{:S(2)}, u32[]{:S(2)}) collective-permute-start(bf16[16,64,128]{2,1,0:T(8,128)(2,1)S(1)} %get-tuple-element.53.refs_5_), channel_id=1, source_target_pairs={{0,4},{4,0},{8,12},{12,8},{16,20},{20,16},{24,28},{28,24},{1,5},{5... | collective-permute-start | bytes 786440 | tf_op jit(solution)/shard_map/ppermute | solution.py:362
  40.6 1.0 %copy-start.3 = (f32[8,256,128]{2,1,0:T(8,128)}, f32[8,256,128]{2,1,0:T(8,128)S(1)}, u32[]{:S(2)}) copy-start(f32[8,256,128]{2,1,0:T(8,128)S(1)} %collective-permute-done.3.refs_3_) | copy-start | bytes 3145732
  41.7 1.0 %copy-start.4 = (f32[8,256,128]{2,1,0:T(8,128)}, f32[8,256,128]{2,1,0:T(8,128)S(1)}, u32[]{:S(2)}) copy-start(f32[8,256,128]{2,1,0:T(8,128)S(1)} %collective-permute-done.4.refs_4_) | copy-start | bytes 3145732
  47.1 8.4 %collective-permute-start.9 = (bf16[4,256,128]{2,1,0:T(8,128)(2,1)}, bf16[4,256,128]{2,1,0:T(8,128)(2,1)S(1)}, u32[]{:S(2)}, u32[]{:S(2)}) collective-permute-start(bf16[4,256,128]{2,1,0:T(8,128)(2,1)} %get-tuple-element.36), channel_id=1, source_target_pairs={{0,8},{4,12},{8,0},{12,4},{16,24},{20,28},{24,16},{28,20},{1,9},{5... | collective-permute-start | bytes 786440 | tf_op jit(solution)/shard_map/ppermute | solution.py:362
  48.4 8.2 %collective-permute-start.10 = (bf16[4,256,128]{2,1,0:T(8,128)(2,1)}, bf16[4,256,128]{2,1,0:T(8,128)(2,1)S(1)}, u32[]{:S(2)}, u32[]{:S(2)}) collective-permute-start(bf16[4,256,128]{2,1,0:T(8,128)(2,1)} %get-tuple-element.37), channel_id=1, source_target_pairs={{0,16},{4,20},{8,24},{12,28},{16,0},{20,4},{24,8},{28,12},{1,17},{... | collective-permute-start | bytes 786440 | tf_op jit(solution)/shard_map/ppermute | solution.py:362
  49.3 12.1 %collective-permute-start.11 = (bf16[4,256,128]{2,1,0:T(8,128)(2,1)}, bf16[4,256,128]{2,1,0:T(8,128)(2,1)S(1)}, u32[]{:S(2)}, u32[]{:S(2)}) collective-permute-start(bf16[4,256,128]{2,1,0:T(8,128)(2,1)} %get-tuple-element.38), channel_id=1, source_target_pairs={{0,24},{4,28},{8,16},{12,20},{16,8},{20,12},{24,0},{28,4},{1,25},{... | collective-permute-start | bytes 786440 | tf_op jit(solution)/shard_map/ppermute | solution.py:362
  50.4 0.8 copy-start.5
  61.4 6.9 %copy-start = (bf16[32,128,128]{2,1,0:T(8,128)(2,1)}, bf16[32,128,128]{2,1,0:T(8,128)(2,1)S(1)}, u32[]{:S(2)}) copy-start(bf16[32,128,128]{2,1,0:T(8,128)(2,1)S(1)} %all-to-all-done) | copy-start | bytes 3145732
  61.4 25.3 %all-to-all-start.1 = ((bf16[32,64,128]{2,1,0:T(8,128)(2,1)}), bf16[32,64,128]{2,1,0:T(8,128)(2,1)S(1)}, u32[]{:S(2)}, u32[]{:S(2)}) async-start(bf16[32,64,128]{2,1,0:T(8,128)(2,1)} %narrow_dpool.1), calls=%async_computation.1 | async-start | bytes 1048576 | tf_op jit(solution)/shard_map/all_to_all | solution.py:395
  68.3 5.5 %copy-start.2 = (f32[4,256,128]{2,1,0:T(8,128)S(1)}, f32[4,256,128]{2,1,0:T(8,128)}, u32[]{:S(2)}) copy-start(f32[4,256,128]{2,1,0:T(8,128)} %get-tuple-element.35.refs_0_) | copy-start | bytes 1572868
  74.0 18.9 %collective-permute-start.12 = (bf16[1,256,128]{2,1,0:T(8,128)(2,1)S(1)}, bf16[1,256,128]{2,1,0:T(8,128)(2,1)S(1)}, u32[]{:S(2)}, u32[]{:S(2)}) collective-permute-start(bf16[1,256,128]{2,1,0:T(8,128)(2,1)S(1)} %get-tuple-element.52), channel_id=1, source_target_pairs={{0,1},{1,0},{2,3},{3,2},{4,5},{5,4},{6,7},{7,6},{8,9},{9,8},{10,11... | collective-permute-start | bytes 196616 | tf_op jit(solution)/shard_map/ppermute | solution.py:362
  75.4 17.5 %collective-permute-start.13 = (bf16[1,256,128]{2,1,0:T(8,128)(2,1)S(1)}, bf16[1,256,128]{2,1,0:T(8,128)(2,1)S(1)}, u32[]{:S(2)}, u32[]{:S(2)}) collective-permute-start(bf16[1,256,128]{2,1,0:T(8,128)(2,1)S(1)} %get-tuple-element.51), channel_id=1, source_target_pairs={{0,2},{1,3},{2,0},{3,1},{4,6},{5,7},{6,4},{7,5},{8,10},{9,11},{10,... | collective-permute-start | bytes 196616 | tf_op jit(solution)/shard_map/ppermute | solution.py:362
  77.5 15.3 %collective-permute-start.14 = (bf16[1,256,128]{2,1,0:T(8,128)(2,1)S(1)}, bf16[1,256,128]{2,1,0:T(8,128)(2,1)S(1)}, u32[]{:S(2)}, u32[]{:S(2)}) collective-permute-start(bf16[1,256,128]{2,1,0:T(8,128)(2,1)S(1)} %get-tuple-element.50), channel_id=1, source_target_pairs={{0,3},{1,2},{2,1},{3,0},{4,7},{5,6},{6,5},{7,4},{8,11},{9,10},{10,... | collective-permute-start | bytes 196616 | tf_op jit(solution)/shard_map/ppermute | solution.py:362
  (1 other events, 0.8 us)
where the time goes:
time: 94.2 us; the launch traced here: 93.6 us
  Pallas kernels  35.5 us (38%)
  starting transfers between devices  28.7 us (30%)
  waiting for transfers between devices  20.9 us (22%)
  local copies, waits for them, and re-layouts  5.16 us (5%)
  other arithmetic  2.44 us (3%)
    ppermute x15, starting transfers between devices, swap(): return lax.ppermute(x, axis, [(d, d ^ bits) for d in range(size)])  14.8 us
    ppermute x15, waiting for transfers between devices, swap(): return lax.ppermute(x, axis, [(d, d ^ bits) for d in range(size)])  11.8 us
    all_to_all x1, waiting for transfers between devices, local(): lax.all_to_all(narrow, AXES, split_axis=0, concat_axis=0, tiled=True)  9.11 us
    pallas_call x2, Pallas kernels, partial_proj(): pl.pallas_call(functools.partial(partial_kernel, len(operands), len(other...  8.87 us
    all_to_all x1, starting transfers between devices, local(): g3_got = lax.all_to_all(g3, AXES, split_axis=0, concat_axis=0, tiled=True)  7.05 us
    all_to_all x1, starting transfers between devices, local(): lax.all_to_all(narrow, AXES, split_axis=0, concat_axis=0, tiled=True)  6.89 us
    pallas_call x1, Pallas kernels, permute(): pl.pallas_call(functools.partial(permute_kernel, slots, pieces), out_shap...  6.46 us
    pallas_call x1, Pallas kernels, wide_sum(): pl.pallas_call(wide_kernel, out_shape=jax.ShapeDtypeStruct((ROWS, WSUM),...  5.48 us
  transfers between devices with their start and end apart: 17, of which 6 were waited for; matrix products, arithmetic and copies ran while one was open for 3% of the time, Pallas kernels for 38%

commit v1 on v0

--- a/solution.py
+++ b/solution.py
@@ -204,7 +204,7 @@
         store.wait()
 
 
-def partial_proj(nodes, lines, q, g12, g3, results, others=(), after=()):
+def partial_proj(nodes, lines, q, g12, g3, results, others=()):
     _, count, _ = q.shape
     blocks, size = nodes.shape[0], lines.shape[0]
     kinds = [jnp.bfloat16 if others and i else jnp.float32 for i in range(results)]
@@ -216,7 +216,7 @@
         grid_spec=pltpu.PrefetchScalarGridSpec(
             num_scalar_prefetch=2,
             grid=(1,),
-            in_specs=[HBM] * (len(operands) + len(others)) + [ANY] * len(after),
+            in_specs=[HBM] * (len(operands) + len(others)),
             out_specs=[HBM] * results,
             scratch_shapes=[pltpu.VMEM((blocks * size, count, x.shape[2]), jnp.bfloat16) for x in operands]
             + [pltpu.VMEM(x.shape, x.dtype) for x in others]
@@ -230,7 +230,7 @@
         compiler_params=params(1),
         cost_estimate=cost(1e7),
         name="partial_proj",
-    )(nodes, lines, *operands, *others, *after)
+    )(nodes, lines, *operands, *others)
 
 
 def count_kernel(index_ref, length_ref, *refs):
@@ -382,8 +382,7 @@
 
     rows, sent = lax.optimization_barrier((rows, sent))
     rows = jnp.concatenate([rows] + [swap(rows, "node", n_node, 2 * d) for d in range(1, n_plane)])
-    hits = count_hits(indices[0].transpose(1, 2, 0), lengths[0].T[:, None, :], after=sent[:1])
-    kept = partial_proj(plane * 2 + node % 2, lines, q, g12, g3, n_plane, got, after=[rows, hits])
+    kept = partial_proj(plane * 2 + node % 2, lines, q, g12, g3, n_plane, got)
     arrived = [swap(kept[d], "node", n_node, 2 * d) for d in range(1, n_plane)]
 
     rows = jnp.concatenate([rows, swap(rows, "node", n_node, 1)])
@@ -391,7 +390,9 @@
     slot_node = slot // n_local ^ node
     slot_place = slot_node % 2 * (slots // 2) + slot_node // 2 * n_local + (slot % n_local ^ loc)
     narrow = narrow_dpool(slot_place, g12, rows, after=kept[:1])
-    narrow, g3_got, arrived = lax.optimization_barrier((narrow, g3_got, arrived))
+    hits = count_hits(indices[0].transpose(1, 2, 0), lengths[0].T[:, None, :], after=[narrow])
+
+    narrow, hits, g3_got, arrived = lax.optimization_barrier((narrow, hits, g3_got, arrived))
     narrow_got = lax.all_to_all(narrow, AXES, split_axis=0, concat_axis=0, tiled=True)
     total = kept[0]
     for term in arrived:

time: 94.2 us -> 89.4 us (0.949)
  waiting for transfers between devices: 20.9 us -> 14.9 us
  starting transfers between devices: 28.7 us -> 30.1 us
    ppermute x15, waiting for transfers between devices: 11.8 us -> 5.75 us  [swap(): return lax.ppermute(x, axis, [(d, d ^ bits) for d in range(size)])]
    ppermute x15, starting transfers between devices: 14.8 us -> 16.1 us  [swap(): return lax.ppermute(x, axis, [(d, d ^ bits) for d in range(size)])]
    unnamed x20 -> x19, local copies, waits for them, and re-layouts: 3.71 us -> 3.61 us
  transfers between devices with their start and end apart: 17 -> 17, of which waited for: 6 -> 5; matrix products, arithmetic and copies ran while one was open for 3% -> 3% of each run, Pallas kernels for 38% -> 40%
where the time goes in v1:
time: 89.4 us; the launch traced here: 88.8 us
  Pallas kernels  35.5 us (40%)
  starting transfers between devices  30.1 us (34%)
  waiting for transfers between devices  14.9 us (17%)
  local copies, waits for them, and re-layouts  5.04 us (6%)
  other arithmetic  2.45 us (3%)
    ppermute x15, starting transfers between devices, swap(): return lax.ppermute(x, axis, [(d, d ^ bits) for d in range(size)])  16.1 us
    all_to_all x1, waiting for transfers between devices, local(): lax.all_to_all(narrow, AXES, split_axis=0, concat_axis=0, tiled=True)  9.11 us
    pallas_call x2, Pallas kernels, partial_proj(): pl.pallas_call(functools.partial(partial_kernel, len(operands), len(other...  8.88 us
    all_to_all x1, starting transfers between devices, local(): g3_got = lax.all_to_all(g3, AXES, split_axis=0, concat_axis=0, tiled=True)  7.05 us
    all_to_all x1, starting transfers between devices, local(): lax.all_to_all(narrow, AXES, split_axis=0, concat_axis=0, tiled=True)  6.96 us
    pallas_call x1, Pallas kernels, permute(): pl.pallas_call(functools.partial(permute_kernel, slots, pieces), out_shap...  6.42 us
    ppermute x15, waiting for transfers between devices, swap(): return lax.ppermute(x, axis, [(d, d ^ bits) for d in range(size)])  5.75 us
    pallas_call x1, Pallas kernels, wide_sum(): pl.pallas_call(wide_kernel, out_shape=jax.ShapeDtypeStruct((ROWS, WSUM),...  5.48 us
  transfers between devices with their start and end apart: 17, of which 5 were waited for; matrix products, arithmetic and copies ran while one was open for 3% of the time, Pallas kernels for 40%

profile of v1, /device:TPU:1, one launch (start us, length us, event | category | flops | bytes accessed | tf_op | source)
XLA Modules:
  0.0 88.8 jit_solution(7002023024772533444)
XLA Ops:
  1.4 4.2 %collective-permute-start.2 = (bf16[1,64,128]{2,1,0:T(8,128)(2,1)S(1)}, bf16[1,64,128]{2,1,0:T(8,128)(2,1)S(1)}, u32[]{:S(2)}, u32[]{:S(2)}) collective-permute-start(bf16[1,64,128]{2,1,0:T(8,128)(2,1)S(1)} %slice.15), channel_id=1, source_target_pairs={{0,3},{1,2},{2,1},{3,0},{4,7},{5,6},{6,5},{7,4},{8,11},{9,10},{10,... | collective-permute-start | bytes 49160 | tf_op jit(solution)/shard_map/ppermute | solution.py:362
  5.8 6.4 %permute_groups.1 = (bf16[32,128,256]{2,1,0:T(8,128)(2,1)}, bf16[32,128,128]{2,1,0:T(8,128)(2,1)}, bf16[32,128,256]{2,1,0:T(8,128)(2,1)}) custom-call(s32[32]{0:T(128)} %assign_ref.1, bf16[128,32,384]{2,1,0:T(8,128)(2,1)} %grad_ref.1, bf16[128,32,256]{2,1,0:T(8,128)(2,1)} %pool_ref.1), custom_call_target="tpu_custom_call" | custom-call | flops 10000000 | bytes 1024 | tf_op jit(solution)/shard_map/permute_groups/pallas_call | solution.py:78
  12.3 7.1 %all-to-all-start = ((bf16[32,128,128]{2,1,0:T(8,128)(2,1)}), bf16[32,128,128]{2,1,0:T(8,128)(2,1)S(1)}, u32[]{:S(2)}, u32[]{:S(2)}) async-start(bf16[32,128,128]{2,1,0:T(8,128)(2,1)} %get-tuple-element.29.refs_2_), calls=%async_computation | async-start | bytes 2097152 | tf_op jit(solution)/shard_map/all_to_all | solution.py:376
  19.9 4.4 %partial_proj.2 = (f32[8,256,128]{2,1,0:T(8,128)}, f32[8,256,128]{2,1,0:T(8,128)}) custom-call(s32[4]{0:T(128)} %get-tuple-element.53.node_ref, s32[4]{0:T(128)} %get-tuple-element.54.line_ref, bf16[32,128,256]{2,1,0:T(8,128)(2,1)} %get-tuple-element.26.refs_0_, bf16[32,128,256]{2,1,0:T(8,128)(2,1)} %get-tuple-element.27.refs_1_.g_ref, ...), custom_call_target="tpu_custom_call" | custom-call | flops 10000000 | bytes 1024 | tf_op jit(solution)/shard_map/partial_proj/pallas_call | solution.py:213
  26.7 1.4 %collective-permute-start.5 = (bf16[4,64,128]{2,1,0:T(8,128)(2,1)S(1)}, bf16[4,64,128]{2,1,0:T(8,128)(2,1)S(1)}, u32[]{:S(2)}, u32[]{:S(2)}) collective-permute-start(bf16[4,64,128]{2,1,0:T(8,128)(2,1)S(1)} %pad_maximum_fusion.1), channel_id=1, source_target_pairs={{0,8},{4,12},{8,0},{12,4},{16,24},{20,28},{24,16},{28,20},{1,9},{5... | collective-permute-start | bytes 196616 | tf_op jit(solution)/shard_map/ppermute | solution.py:362
  28.0 1.2 %collective-permute-start.6 = (bf16[4,64,128]{2,1,0:T(8,128)(2,1)S(1)}, bf16[4,64,128]{2,1,0:T(8,128)(2,1)S(1)}, u32[]{:S(2)}, u32[]{:S(2)}) collective-permute-start(bf16[4,64,128]{2,1,0:T(8,128)(2,1)S(1)} %pad_maximum_fusion.1), channel_id=1, source_target_pairs={{0,16},{4,20},{8,24},{12,28},{16,0},{20,4},{24,8},{28,12},{1,17},{... | collective-permute-start | bytes 196616 | tf_op jit(solution)/shard_map/ppermute | solution.py:362
  29.3 1.5 %collective-permute-done.5 = bf16[4,64,128]{2,1,0:T(8,128)(2,1)S(1)} collective-permute-done((bf16[4,64,128]{2,1,0:T(8,128)(2,1)S(1)}, bf16[4,64,128]{2,1,0:T(8,128)(2,1)S(1)}, u32[]{:S(2)}, u32[]{:S(2)}) %collective-permute-start.5) | collective-permute-done | bytes 65568 | tf_op jit(solution)/shard_map/ppermute | solution.py:362
  30.8 1.4 %collective-permute-done.6 = bf16[4,64,128]{2,1,0:T(8,128)(2,1)S(1)} collective-permute-done((bf16[4,64,128]{2,1,0:T(8,128)(2,1)S(1)}, bf16[4,64,128]{2,1,0:T(8,128)(2,1)S(1)}, u32[]{:S(2)}, u32[]{:S(2)}) %collective-permute-start.6) | collective-permute-done | bytes 65568 | tf_op jit(solution)/shard_map/ppermute | solution.py:362
  32.2 1.6 %collective-permute-done.7 = bf16[4,64,128]{2,1,0:T(8,128)(2,1)S(1)} collective-permute-done((bf16[4,64,128]{2,1,0:T(8,128)(2,1)S(1)}, bf16[4,64,128]{2,1,0:T(8,128)(2,1)S(1)}, u32[]{:S(2)}, u32[]{:S(2)}) %collective-permute-start.7) | collective-permute-done | bytes 65568 | tf_op jit(solution)/shard_map/ppermute | solution.py:362
  33.8 2.1 %collective-permute-start.8 = (bf16[16,64,128]{2,1,0:T(8,128)(2,1)S(1)}, bf16[16,64,128]{2,1,0:T(8,128)(2,1)S(1)}, u32[]{:S(2)}, u32[]{:S(2)}) collective-permute-start(bf16[16,64,128]{2,1,0:T(8,128)(2,1)S(1)} %pad_maximum_fusion), channel_id=1, source_target_pairs={{0,4},{4,0},{8,12},{12,8},{16,20},{20,16},{24,28},{28,24},{1,5},{5... | collective-permute-start | bytes 786440 | tf_op jit(solution)/shard_map/ppermute | solution.py:362
  35.9 1.0 %copy-done.3 = f32[8,256,128]{2,1,0:T(8,128)} copy-done((f32[8,256,128]{2,1,0:T(8,128)}, f32[8,256,128]{2,1,0:T(8,128)S(1)}, u32[]{:S(2)}) %copy-start.3) | copy-done | bytes 1048600
  36.9 1.0 %copy-done.4 = f32[8,256,128]{2,1,0:T(8,128)} copy-done((f32[8,256,128]{2,1,0:T(8,128)}, f32[8,256,128]{2,1,0:T(8,128)S(1)}, u32[]{:S(2)}) %copy-start.4) | copy-done | bytes 1048600
  37.8 4.4 %partial_proj.3 = (f32[4,256,128]{2,1,0:T(8,128)}, bf16[4,256,128]{2,1,0:T(8,128)(2,1)}, bf16[4,256,128]{2,1,0:T(8,128)(2,1)}, bf16[4,256,128]{2,1,0:T(8,128)(2,1)}) custom-call(s32[4]{0:T(128)} %fusion.5.node_ref, s32[4]{0:T(128)} %get-tuple-element.54.line_ref, bf16[32,128,256]{2,1,0:T(8,128)(2,1)} %get-tuple-element.26.refs_0_, ...), custom_call_target="tpu_custom_call" | custom-call | flops 10000000 | bytes 1024 | tf_op jit(solution)/shard_map/partial_proj/pallas_call | solution.py:213
  42.3 1.0 %collective-permute-start.9 = (bf16[4,256,128]{2,1,0:T(8,128)(2,1)}, bf16[4,256,128]{2,1,0:T(8,128)(2,1)S(1)}, u32[]{:S(2)}, u32[]{:S(2)}) collective-permute-start(bf16[4,256,128]{2,1,0:T(8,128)(2,1)} %get-tuple-element.35), channel_id=1, source_target_pairs={{0,8},{4,12},{8,0},{12,4},{16,24},{20,28},{24,16},{28,20},{1,9},{5... | collective-permute-start | bytes 786440 | tf_op jit(solution)/shard_map/ppermute | solution.py:362
  43.7 1.3 %collective-permute-start.11 = (bf16[4,256,128]{2,1,0:T(8,128)(2,1)}, bf16[4,256,128]{2,1,0:T(8,128)(2,1)S(1)}, u32[]{:S(2)}, u32[]{:S(2)}) collective-permute-start(bf16[4,256,128]{2,1,0:T(8,128)(2,1)} %get-tuple-element.37), channel_id=1, source_target_pairs={{0,24},{4,28},{8,16},{12,20},{16,8},{20,12},{24,0},{28,4},{1,25},{... | collective-permute-start | bytes 786440 | tf_op jit(solution)/shard_map/ppermute | solution.py:362
  45.9 4.4 %narrow_dpool.1.refs_0_ = bf16[32,64,128]{2,1,0:T(8,128)(2,1)} custom-call(s32[32]{0:T(128)} %fusion.1.place_ref, bf16[32,128,256]{2,1,0:T(8,128)(2,1)} %get-tuple-element.27.refs_1_.g_ref, bf16[32,64,128]{2,1,0:T(8,128)(2,1)} %copy-done.5, f32[4,256,128]{2,1,0:T(8,128)} %get-tuple-element.32.refs_0_), custom_call_target="tpu_custom_call" | custom-call | flops 10000000 | bytes 1024 | tf_op jit(solution)/shard_map/narrow_dpool/pallas_call | solution.py:139
  50.2 4.9 %count_hits.1.hits_ref = s32[3,64,4096]{2,1,0:T(8,128)} custom-call(s32[3,8,4096]{2,1,0:T(8,128)} %bitcast.13, s32[3,1,4096]{2,1,0:T(1,128)} %broadcast_in_dim.6.length_ref, bf16[32,64,128]{2,1,0:T(8,128)(2,1)} %narrow_dpool.1.refs_0_), custom_call_target="tpu_custom_call" | custom-call | flops 10000000 | bytes 1024 | tf_op jit(solution)/shard_map/count_hits/pallas_call | solution.py:261
  55.2 1.3 %collective-permute-done.11 = bf16[4,256,128]{2,1,0:T(8,128)(2,1)S(1)} collective-permute-done((bf16[4,256,128]{2,1,0:T(8,128)(2,1)}, bf16[4,256,128]{2,1,0:T(8,128)(2,1)S(1)}, u32[]{:S(2)}, u32[]{:S(2)}) %collective-permute-start.11) | collective-permute-done | bytes 262176 | tf_op jit(solution)/shard_map/ppermute | solution.py:362
  56.5 7.0 %all-to-all-start.1 = ((bf16[32,64,128]{2,1,0:T(8,128)(2,1)}), bf16[32,64,128]{2,1,0:T(8,128)(2,1)S(1)}, u32[]{:S(2)}, u32[]{:S(2)}) async-start(bf16[32,64,128]{2,1,0:T(8,128)(2,1)} %narrow_dpool.1.refs_0_), calls=%async_computation.1 | async-start | bytes 1048576 | tf_op jit(solution)/shard_map/all_to_all | solution.py:396
  63.5 5.5 %wide_sum.1.wide_ref = f32[512,256]{1,0:T(8,128)} custom-call(s32[3,64,4096]{2,1,0:T(8,128)} %count_hits.1.hits_ref, bf16[4096,128]{1,0:T(8,128)(2,1)} %bitcast.11, bf16[256,128]{1,0:T(8,128)(2,1)} %bitcast.15), custom_call_target="tpu_custom_call" | custom-call | flops 10000000 | bytes 1024 | tf_op jit(solution)/shard_map/wide_sum/pallas_call | solution.py:299
  69.1 1.5 %collective-permute-start.12 = (bf16[1,256,128]{2,1,0:T(8,128)(2,1)S(1)}, bf16[1,256,128]{2,1,0:T(8,128)(2,1)S(1)}, u32[]{:S(2)}, u32[]{:S(2)}) collective-permute-start(bf16[1,256,128]{2,1,0:T(8,128)(2,1)S(1)} %get-tuple-element.52), channel_id=1, source_target_pairs={{0,1},{1,0},{2,3},{3,2},{4,5},{5,4},{6,7},{7,6},{8,9},{9,8},{10,11... | collective-permute-start | bytes 196616 | tf_op jit(solution)/shard_map/ppermute | solution.py:362
  70.6 2.1 %collective-permute-start.13 = (bf16[1,256,128]{2,1,0:T(8,128)(2,1)S(1)}, bf16[1,256,128]{2,1,0:T(8,128)(2,1)S(1)}, u32[]{:S(2)}, u32[]{:S(2)}) collective-permute-start(bf16[1,256,128]{2,1,0:T(8,128)(2,1)S(1)} %get-tuple-element.51), channel_id=1, source_target_pairs={{0,2},{1,3},{2,0},{3,1},{4,6},{5,7},{6,4},{7,5},{8,10},{9,11},{10,... | collective-permute-start | bytes 196616 | tf_op jit(solution)/shard_map/ppermute | solution.py:362
  72.7 9.1 %all-to-all-done.1.d_ref = bf16[32,64,128]{2,1,0:T(8,128)(2,1)S(1)} async-done(((bf16[32,64,128]{2,1,0:T(8,128)(2,1)}), bf16[32,64,128]{2,1,0:T(8,128)(2,1)S(1)}, u32[]{:S(2)}, u32[]{:S(2)}) %all-to-all-start.1) | async-done | bytes 524320 | tf_op jit(solution)/shard_map/all_to_all | solution.py:396
  82.7 5.4 %narrow_sum.1 = f32[512,256]{1,0:T(8,128)} custom-call(s32[3,64,4096]{2,1,0:T(8,128)} %count_hits.1.hits_ref, bf16[32,64,128]{2,1,0:T(8,128)(2,1)} %copy-done.1, f32[512,256]{1,0:T(8,128)} %wide_sum.1.wide_ref), custom_call_target="tpu_custom_call", output_to_operand_aliasing={{}: (2, {})} | custom-call | flops 10000000 | bytes 1024 | tf_op jit(solution)/shard_map/narrow_sum/pallas_call | solution.py:343
  (48 shorter events, 7.0 us)
Async XLA Ops:
  1.4 10.9 %collective-permute-start.2 = (bf16[1,64,128]{2,1,0:T(8,128)(2,1)S(1)}, bf16[1,64,128]{2,1,0:T(8,128)(2,1)S(1)}, u32[]{:S(2)}, u32[]{:S(2)}) collective-permute-start(bf16[1,64,128]{2,1,0:T(8,128)(2,1)S(1)} %slice.15), channel_id=1, source_target_pairs={{0,3},{1,2},{2,1},{3,0},{4,7},{5,6},{6,5},{7,4},{8,11},{9,10},{10,... | collective-permute-start | bytes 49160 | tf_op jit(solution)/shard_map/ppermute | solution.py:362
  5.5 6.7 %collective-permute-start.1 = (bf16[1,64,128]{2,1,0:T(8,128)(2,1)S(1)}, bf16[1,64,128]{2,1,0:T(8,128)(2,1)S(1)}, u32[]{:S(2)}, u32[]{:S(2)}) collective-permute-start(bf16[1,64,128]{2,1,0:T(8,128)(2,1)S(1)} %slice.15), channel_id=1, source_target_pairs={{0,2},{1,3},{2,0},{3,1},{4,6},{5,7},{6,4},{7,5},{8,10},{9,11},{10,... | collective-permute-start | bytes 49160 | tf_op jit(solution)/shard_map/ppermute | solution.py:362
  5.5 6.7 %collective-permute-start = (bf16[1,64,128]{2,1,0:T(8,128)(2,1)S(1)}, bf16[1,64,128]{2,1,0:T(8,128)(2,1)S(1)}, u32[]{:S(2)}, u32[]{:S(2)}) collective-permute-start(bf16[1,64,128]{2,1,0:T(8,128)(2,1)S(1)} %slice.15), channel_id=1, source_target_pairs={{0,1},{1,0},{2,3},{3,2},{4,5},{5,4},{6,7},{7,6},{8,9},{9,8},{10,11... | collective-permute-start | bytes 49160 | tf_op jit(solution)/shard_map/ppermute | solution.py:362
  12.3 44.2 %all-to-all-start = ((bf16[32,128,128]{2,1,0:T(8,128)(2,1)}), bf16[32,128,128]{2,1,0:T(8,128)(2,1)S(1)}, u32[]{:S(2)}, u32[]{:S(2)}) async-start(bf16[32,128,128]{2,1,0:T(8,128)(2,1)} %get-tuple-element.29.refs_2_), calls=%async_computation | async-start | bytes 2097152 | tf_op jit(solution)/shard_map/all_to_all | solution.py:376
  19.9 5.0 %copy-start.6 = (s32[1,4096,3]{1,0,2:T(1,128)S(1)}, s32[1,4096,3]{1,0,2:T(1,128)}, u32[]{:S(2)}) copy-start(s32[1,4096,3]{1,0,2:T(1,128)} %param.11) | copy-start | bytes 147460
  24.3 11.6 %collective-permute-start.3 = (f32[8,256,128]{2,1,0:T(8,128)}, f32[8,256,128]{2,1,0:T(8,128)S(1)}, u32[]{:S(2)}, u32[]{:S(2)}) collective-permute-start(f32[8,256,128]{2,1,0:T(8,128)} %get-tuple-element.30), channel_id=1, source_target_pairs={{0,4},{4,0},{8,12},{12,8},{16,20},{20,16},{24,28},{28,24},{1,5},{5... | collective-permute-start | bytes 3145736 | tf_op jit(solution)/shard_map/ppermute | solution.py:362
  24.7 11.3 %collective-permute-start.4 = (f32[8,256,128]{2,1,0:T(8,128)}, f32[8,256,128]{2,1,0:T(8,128)S(1)}, u32[]{:S(2)}, u32[]{:S(2)}) collective-permute-start(f32[8,256,128]{2,1,0:T(8,128)} %get-tuple-element.31), channel_id=1, source_target_pairs={{0,4},{4,0},{8,12},{12,8},{16,20},{20,16},{24,28},{28,24},{1,5},{5... | collective-permute-start | bytes 3145736 | tf_op jit(solution)/shard_map/ppermute | solution.py:362
  26.7 4.1 %collective-permute-start.5 = (bf16[4,64,128]{2,1,0:T(8,128)(2,1)S(1)}, bf16[4,64,128]{2,1,0:T(8,128)(2,1)S(1)}, u32[]{:S(2)}, u32[]{:S(2)}) collective-permute-start(bf16[4,64,128]{2,1,0:T(8,128)(2,1)S(1)} %pad_maximum_fusion.1), channel_id=1, source_target_pairs={{0,8},{4,12},{8,0},{12,4},{16,24},{20,28},{24,16},{28,20},{1,9},{5... | collective-permute-start | bytes 196616 | tf_op jit(solution)/shard_map/ppermute | solution.py:362
  28.0 4.1 %collective-permute-start.6 = (bf16[4,64,128]{2,1,0:T(8,128)(2,1)S(1)}, bf16[4,64,128]{2,1,0:T(8,128)(2,1)S(1)}, u32[]{:S(2)}, u32[]{:S(2)}) collective-permute-start(bf16[4,64,128]{2,1,0:T(8,128)(2,1)S(1)} %pad_maximum_fusion.1), channel_id=1, source_target_pairs={{0,16},{4,20},{8,24},{12,28},{16,0},{20,4},{24,8},{28,12},{1,17},{... | collective-permute-start | bytes 196616 | tf_op jit(solution)/shard_map/ppermute | solution.py:362
  29.2 4.5 %collective-permute-start.7 = (bf16[4,64,128]{2,1,0:T(8,128)(2,1)S(1)}, bf16[4,64,128]{2,1,0:T(8,128)(2,1)S(1)}, u32[]{:S(2)}, u32[]{:S(2)}) collective-permute-start(bf16[4,64,128]{2,1,0:T(8,128)(2,1)S(1)} %pad_maximum_fusion.1), channel_id=1, source_target_pairs={{0,24},{4,28},{8,16},{12,20},{16,8},{20,12},{24,0},{28,4},{1,25},{... | collective-permute-start | bytes 196616 | tf_op jit(solution)/shard_map/ppermute | solution.py:362
  33.8 11.2 %collective-permute-start.8 = (bf16[16,64,128]{2,1,0:T(8,128)(2,1)S(1)}, bf16[16,64,128]{2,1,0:T(8,128)(2,1)S(1)}, u32[]{:S(2)}, u32[]{:S(2)}) collective-permute-start(bf16[16,64,128]{2,1,0:T(8,128)(2,1)S(1)} %pad_maximum_fusion), channel_id=1, source_target_pairs={{0,4},{4,0},{8,12},{12,8},{16,20},{20,16},{24,28},{28,24},{1,5},{5... | collective-permute-start | bytes 786440 | tf_op jit(solution)/shard_map/ppermute | solution.py:362
  35.9 1.0 %copy-start.3 = (f32[8,256,128]{2,1,0:T(8,128)}, f32[8,256,128]{2,1,0:T(8,128)S(1)}, u32[]{:S(2)}) copy-start(f32[8,256,128]{2,1,0:T(8,128)S(1)} %collective-permute-done.3.refs_3_) | copy-start | bytes 3145732
  36.9 1.0 %copy-start.4 = (f32[8,256,128]{2,1,0:T(8,128)}, f32[8,256,128]{2,1,0:T(8,128)S(1)}, u32[]{:S(2)}) copy-start(f32[8,256,128]{2,1,0:T(8,128)S(1)} %collective-permute-done.4.refs_4_) | copy-start | bytes 3145732
  42.3 12.9 %collective-permute-start.9 = (bf16[4,256,128]{2,1,0:T(8,128)(2,1)}, bf16[4,256,128]{2,1,0:T(8,128)(2,1)S(1)}, u32[]{:S(2)}, u32[]{:S(2)}) collective-permute-start(bf16[4,256,128]{2,1,0:T(8,128)(2,1)} %get-tuple-element.35), channel_id=1, source_target_pairs={{0,8},{4,12},{8,0},{12,4},{16,24},{20,28},{24,16},{28,20},{1,9},{5... | collective-permute-start | bytes 786440 | tf_op jit(solution)/shard_map/ppermute | solution.py:362
  43.3 11.9 %collective-permute-start.10 = (bf16[4,256,128]{2,1,0:T(8,128)(2,1)}, bf16[4,256,128]{2,1,0:T(8,128)(2,1)S(1)}, u32[]{:S(2)}, u32[]{:S(2)}) collective-permute-start(bf16[4,256,128]{2,1,0:T(8,128)(2,1)} %get-tuple-element.36), channel_id=1, source_target_pairs={{0,16},{4,20},{8,24},{12,28},{16,0},{20,4},{24,8},{28,12},{1,17},{... | collective-permute-start | bytes 786440 | tf_op jit(solution)/shard_map/ppermute | solution.py:362
  43.7 12.7 %collective-permute-start.11 = (bf16[4,256,128]{2,1,0:T(8,128)(2,1)}, bf16[4,256,128]{2,1,0:T(8,128)(2,1)S(1)}, u32[]{:S(2)}, u32[]{:S(2)}) collective-permute-start(bf16[4,256,128]{2,1,0:T(8,128)(2,1)} %get-tuple-element.37), channel_id=1, source_target_pairs={{0,24},{4,28},{8,16},{12,20},{16,8},{20,12},{24,0},{28,4},{1,25},{... | collective-permute-start | bytes 786440 | tf_op jit(solution)/shard_map/ppermute | solution.py:362
  45.1 0.8 copy-start.5
  56.5 7.0 %copy-start = (bf16[32,128,128]{2,1,0:T(8,128)(2,1)}, bf16[32,128,128]{2,1,0:T(8,128)(2,1)S(1)}, u32[]{:S(2)}) copy-start(bf16[32,128,128]{2,1,0:T(8,128)(2,1)S(1)} %all-to-all-done) | copy-start | bytes 3145732
  56.5 25.4 %all-to-all-start.1 = ((bf16[32,64,128]{2,1,0:T(8,128)(2,1)}), bf16[32,64,128]{2,1,0:T(8,128)(2,1)S(1)}, u32[]{:S(2)}, u32[]{:S(2)}) async-start(bf16[32,64,128]{2,1,0:T(8,128)(2,1)} %narrow_dpool.1.refs_0_), calls=%async_computation.1 | async-start | bytes 1048576 | tf_op jit(solution)/shard_map/all_to_all | solution.py:396
  63.4 5.5 %copy-start.2 = (f32[4,256,128]{2,1,0:T(8,128)S(1)}, f32[4,256,128]{2,1,0:T(8,128)}, u32[]{:S(2)}) copy-start(f32[4,256,128]{2,1,0:T(8,128)} %get-tuple-element.32.refs_0_) | copy-start | bytes 1572868
  69.1 18.9 %collective-permute-start.12 = (bf16[1,256,128]{2,1,0:T(8,128)(2,1)S(1)}, bf16[1,256,128]{2,1,0:T(8,128)(2,1)S(1)}, u32[]{:S(2)}, u32[]{:S(2)}) collective-permute-start(bf16[1,256,128]{2,1,0:T(8,128)(2,1)S(1)} %get-tuple-element.52), channel_id=1, source_target_pairs={{0,1},{1,0},{2,3},{3,2},{4,5},{5,4},{6,7},{7,6},{8,9},{9,8},{10,11... | collective-permute-start | bytes 196616 | tf_op jit(solution)/shard_map/ppermute | solution.py:362
  70.6 17.5 %collective-permute-start.13 = (bf16[1,256,128]{2,1,0:T(8,128)(2,1)S(1)}, bf16[1,256,128]{2,1,0:T(8,128)(2,1)S(1)}, u32[]{:S(2)}, u32[]{:S(2)}) collective-permute-start(bf16[1,256,128]{2,1,0:T(8,128)(2,1)S(1)} %get-tuple-element.51), channel_id=1, source_target_pairs={{0,2},{1,3},{2,0},{3,1},{4,6},{5,7},{6,4},{7,5},{8,10},{9,11},{10,... | collective-permute-start | bytes 196616 | tf_op jit(solution)/shard_map/ppermute | solution.py:362
  72.7 15.3 %collective-permute-start.14 = (bf16[1,256,128]{2,1,0:T(8,128)(2,1)S(1)}, bf16[1,256,128]{2,1,0:T(8,128)(2,1)S(1)}, u32[]{:S(2)}, u32[]{:S(2)}) collective-permute-start(bf16[1,256,128]{2,1,0:T(8,128)(2,1)S(1)} %get-tuple-element.50), channel_id=1, source_target_pairs={{0,3},{1,2},{2,1},{3,0},{4,7},{5,6},{6,5},{7,4},{8,11},{9,10},{10,... | collective-permute-start | bytes 196616 | tf_op jit(solution)/shard_map/ppermute | solution.py:362
  81.8 0.8 copy-start.1

commit v2 on v1

--- a/solution.py
+++ b/solution.py
@@ -216,7 +216,7 @@
         grid_spec=pltpu.PrefetchScalarGridSpec(
             num_scalar_prefetch=2,
             grid=(1,),
-            in_specs=[HBM] * (len(operands) + len(others)),
+            in_specs=[HBM] * len(operands) + [ANY] * len(others),
             out_specs=[HBM] * results,
             scratch_shapes=[pltpu.VMEM((blocks * size, count, x.shape[2]), jnp.bfloat16) for x in operands]
             + [pltpu.VMEM(x.shape, x.dtype) for x in others]
@@ -383,7 +383,6 @@
     rows, sent = lax.optimization_barrier((rows, sent))
     rows = jnp.concatenate([rows] + [swap(rows, "node", n_node, 2 * d) for d in range(1, n_plane)])
     kept = partial_proj(plane * 2 + node % 2, lines, q, g12, g3, n_plane, got)
-    arrived = [swap(kept[d], "node", n_node, 2 * d) for d in range(1, n_plane)]
 
     rows = jnp.concatenate([rows, swap(rows, "node", n_node, 1)])
     slot = jnp.arange(slots, dtype=jnp.int32)
@@ -392,11 +391,11 @@
     narrow = narrow_dpool(slot_place, g12, rows, after=kept[:1])
     hits = count_hits(indices[0].transpose(1, 2, 0), lengths[0].T[:, None, :], after=[narrow])
 
-    narrow, hits, g3_got, arrived = lax.optimization_barrier((narrow, hits, g3_got, arrived))
+    narrow, g3_got, kept = lax.optimization_barrier((narrow, g3_got, kept))
     narrow_got = lax.all_to_all(narrow, AXES, split_axis=0, concat_axis=0, tiled=True)
     total = kept[0]
-    for term in arrived:
-        total = total + term.astype(jnp.float32)
+    for d in range(1, n_plane):
+        total = total + swap(kept[d], "node", n_node, 2 * d).astype(jnp.float32)
     wide = wide_sum(hits, g3_got.reshape(-1, PD), proj[0])
     total, wide = lax.optimization_barrier((total, wide))
     rounded = total.astype(jnp.bfloat16)

time: 89.4 us -> 86 us (0.962)
  the two profiles are of different devices: /device:TPU:1 before, /device:TPU:0 now
where the time goes in v2:
time: 86 us; the launch traced here: 85.3 us
  Pallas kernels  35.5 us (41%)
  starting transfers between devices  29.6 us (34%)
  waiting for transfers between devices  12.5 us (15%)
  local copies, waits for them, and re-layouts  4.31 us (5%)
  other arithmetic  2.52 us (3%)
  between operations  0.91 us (1%)
    ppermute x15, starting transfers between devices, swap(): return lax.ppermute(x, axis, [(d, d ^ bits) for d in range(size)])  17.8 us
    ppermute x15, waiting for transfers between devices, swap(): return lax.ppermute(x, axis, [(d, d ^ bits) for d in range(size)])  12.5 us
    pallas_call x2, Pallas kernels, partial_proj(): pl.pallas_call(functools.partial(partial_kernel, len(operands), len(other...  8.73 us
    pallas_call x1, Pallas kernels, permute(): pl.pallas_call(functools.partial(permute_kernel, slots, pieces), out_shap...  6.5 us
    all_to_all x1, starting transfers between devices, local(): g3_got = lax.all_to_all(g3, AXES, split_axis=0, concat_axis=0, tiled=True)  6.07 us
    all_to_all x1, starting transfers between devices, local(): lax.all_to_all(narrow, AXES, split_axis=0, concat_axis=0, tiled=True)  5.77 us
    pallas_call x1, Pallas kernels, wide_sum(): pl.pallas_call(wide_kernel, out_shape=jax.ShapeDtypeStruct((ROWS, WSUM),...  5.47 us
    pallas_call x1, Pallas kernels, narrow_sum(): pl.pallas_call(narrow_sum_kernel, out_shape=jax.ShapeDtypeStruct((ROWS, W...  5.39 us
  transfers between devices with their start and end apart: 17, of which 6 were waited for; matrix products, arithmetic and copies ran while one was open for 3% of the time, Pallas kernels for 42%

profile of v2, /device:TPU:0, one launch (start us, length us, event | category | flops | bytes accessed | tf_op | source)
XLA Modules:
  0.0 85.3 jit_solution(12470183189653862842)
XLA Ops:
  1.4 5.0 %collective-permute-start.2 = (bf16[1,64,128]{2,1,0:T(8,128)(2,1)S(1)}, bf16[1,64,128]{2,1,0:T(8,128)(2,1)S(1)}, u32[]{:S(2)}, u32[]{:S(2)}) collective-permute-start(bf16[1,64,128]{2,1,0:T(8,128)(2,1)S(1)} %slice.15), channel_id=1, source_target_pairs={{0,3},{1,2},{2,1},{3,0},{4,7},{5,6},{6,5},{7,4},{8,11},{9,10},{10,... | collective-permute-start | bytes 49160 | tf_op jit(solution)/shard_map/ppermute | solution.py:362
  7.0 6.5 %permute_groups.1 = (bf16[32,128,256]{2,1,0:T(8,128)(2,1)}, bf16[32,128,128]{2,1,0:T(8,128)(2,1)}, bf16[32,128,256]{2,1,0:T(8,128)(2,1)}) custom-call(s32[32]{0:T(128)} %assign_ref.1, bf16[128,32,384]{2,1,0:T(8,128)(2,1)} %grad_ref.1, bf16[128,32,256]{2,1,0:T(8,128)(2,1)} %pool_ref.1), custom_call_target="tpu_custom_call" | custom-call | flops 10000000 | bytes 1024 | tf_op jit(solution)/shard_map/permute_groups/pallas_call | solution.py:78
  13.5 6.1 %all-to-all-start = ((bf16[32,128,128]{2,1,0:T(8,128)(2,1)}), bf16[32,128,128]{2,1,0:T(8,128)(2,1)S(1)}, u32[]{:S(2)}, u32[]{:S(2)}) async-start(bf16[32,128,128]{2,1,0:T(8,128)(2,1)} %get-tuple-element.30.refs_2_), calls=%async_computation | async-start | bytes 2097152 | tf_op jit(solution)/shard_map/all_to_all | solution.py:376
  20.2 4.3 %partial_proj.2 = (f32[8,256,128]{2,1,0:T(8,128)}, f32[8,256,128]{2,1,0:T(8,128)}) custom-call(s32[4]{0:T(128)} %get-tuple-element.54.node_ref, s32[4]{0:T(128)} %get-tuple-element.53.line_ref, bf16[32,128,256]{2,1,0:T(8,128)(2,1)} %get-tuple-element.29.refs_0_, bf16[32,128,256]{2,1,0:T(8,128)(2,1)} %get-tuple-element.26.refs_1_.g_ref, ...), custom_call_target="tpu_custom_call" | custom-call | flops 10000000 | bytes 1024 | tf_op jit(solution)/shard_map/partial_proj/pallas_call | solution.py:213
  26.2 1.8 %collective-permute-start.3 = (bf16[4,64,128]{2,1,0:T(8,128)(2,1)S(1)}, bf16[4,64,128]{2,1,0:T(8,128)(2,1)S(1)}, u32[]{:S(2)}, u32[]{:S(2)}) collective-permute-start(bf16[4,64,128]{2,1,0:T(8,128)(2,1)S(1)} %pad_maximum_fusion.1), channel_id=1, source_target_pairs={{0,8},{4,12},{8,0},{12,4},{16,24},{20,28},{24,16},{28,20},{1,9},{5... | collective-permute-start | bytes 196616 | tf_op jit(solution)/shard_map/ppermute | solution.py:362
  27.9 1.5 %collective-permute-start.4 = (bf16[4,64,128]{2,1,0:T(8,128)(2,1)S(1)}, bf16[4,64,128]{2,1,0:T(8,128)(2,1)S(1)}, u32[]{:S(2)}, u32[]{:S(2)}) collective-permute-start(bf16[4,64,128]{2,1,0:T(8,128)(2,1)S(1)} %pad_maximum_fusion.1), channel_id=1, source_target_pairs={{0,16},{4,20},{8,24},{12,28},{16,0},{20,4},{24,8},{28,12},{1,17},{... | collective-permute-start | bytes 196616 | tf_op jit(solution)/shard_map/ppermute | solution.py:362
  29.6 1.7 %collective-permute-done.3 = bf16[4,64,128]{2,1,0:T(8,128)(2,1)S(1)} collective-permute-done((bf16[4,64,128]{2,1,0:T(8,128)(2,1)S(1)}, bf16[4,64,128]{2,1,0:T(8,128)(2,1)S(1)}, u32[]{:S(2)}, u32[]{:S(2)}) %collective-permute-start.3) | collective-permute-done | bytes 65568 | tf_op jit(solution)/shard_map/ppermute | solution.py:362
  31.3 3.3 %collective-permute-done.4 = bf16[4,64,128]{2,1,0:T(8,128)(2,1)S(1)} collective-permute-done((bf16[4,64,128]{2,1,0:T(8,128)(2,1)S(1)}, bf16[4,64,128]{2,1,0:T(8,128)(2,1)S(1)}, u32[]{:S(2)}, u32[]{:S(2)}) %collective-permute-start.4) | collective-permute-done | bytes 65568 | tf_op jit(solution)/shard_map/ppermute | solution.py:362
  35.2 1.5 %collective-permute-done.6 = bf16[16,64,128]{2,1,0:T(8,128)(2,1)S(1)} collective-permute-done((bf16[16,64,128]{2,1,0:T(8,128)(2,1)S(1)}, bf16[16,64,128]{2,1,0:T(8,128)(2,1)S(1)}, u32[]{:S(2)}, u32[]{:S(2)}) %collective-permute-start.6) | collective-permute-done | bytes 262176 | tf_op jit(solution)/shard_map/ppermute | solution.py:362
  36.8 1.0 %copy-done.3 = f32[8,256,128]{2,1,0:T(8,128)} copy-done((f32[8,256,128]{2,1,0:T(8,128)}, f32[8,256,128]{2,1,0:T(8,128)S(1)}, u32[]{:S(2)}) %copy-start.3) | copy-done | bytes 1048600
  37.8 1.0 %copy-done.4 = f32[8,256,128]{2,1,0:T(8,128)} copy-done((f32[8,256,128]{2,1,0:T(8,128)}, f32[8,256,128]{2,1,0:T(8,128)S(1)}, u32[]{:S(2)}) %copy-start.4) | copy-done | bytes 1048600
  38.8 4.4 %partial_proj.3 = (f32[4,256,128]{2,1,0:T(8,128)}, bf16[4,256,128]{2,1,0:T(8,128)(2,1)}, bf16[4,256,128]{2,1,0:T(8,128)(2,1)}, bf16[4,256,128]{2,1,0:T(8,128)(2,1)}) custom-call(s32[4]{0:T(128)} %fusion.5.node_ref, s32[4]{0:T(128)} %get-tuple-element.53.line_ref, bf16[32,128,256]{2,1,0:T(8,128)(2,1)} %get-tuple-element.29.refs_0_, ...), custom_call_target="tpu_custom_call" | custom-call | flops 10000000 | bytes 1024 | tf_op jit(solution)/shard_map/partial_proj/pallas_call | solution.py:213
  43.3 4.5 %narrow_dpool.1.refs_0_ = bf16[32,64,128]{2,1,0:T(8,128)(2,1)} custom-call(s32[32]{0:T(128)} %fusion.1.place_ref, bf16[32,128,256]{2,1,0:T(8,128)(2,1)} %get-tuple-element.26.refs_1_.g_ref, bf16[32,64,128]{2,1,0:T(8,128)(2,1)} %copy-done.5, f32[4,256,128]{2,1,0:T(8,128)} %get-tuple-element.38.refs_0_), custom_call_target="tpu_custom_call" | custom-call | flops 10000000 | bytes 1024 | tf_op jit(solution)/shard_map/narrow_dpool/pallas_call | solution.py:139
  47.8 5.8 %all-to-all-start.1 = ((bf16[32,64,128]{2,1,0:T(8,128)(2,1)}), bf16[32,64,128]{2,1,0:T(8,128)(2,1)S(1)}, u32[]{:S(2)}, u32[]{:S(2)}) async-start(bf16[32,64,128]{2,1,0:T(8,128)(2,1)} %narrow_dpool.1.refs_0_), calls=%async_computation.1 | async-start | bytes 1048576 | tf_op jit(solution)/shard_map/all_to_all | solution.py:395
  53.5 2.7 %collective-permute-start.11 = (bf16[4,256,128]{2,1,0:T(8,128)(2,1)S(1)}, bf16[4,256,128]{2,1,0:T(8,128)(2,1)S(1)}, u32[]{:S(2)}, u32[]{:S(2)}) collective-permute-start(bf16[4,256,128]{2,1,0:T(8,128)(2,1)S(1)} %copy-done.9), channel_id=1, source_target_pairs={{0,24},{4,28},{8,16},{12,20},{16,8},{20,12},{24,0},{28,4},{1,25},{... | collective-permute-start | bytes 786440 | tf_op jit(solution)/shard_map/ppermute | solution.py:362
  57.8 4.9 %count_hits.1.hits_ref = s32[3,64,4096]{2,1,0:T(8,128)} custom-call(s32[3,8,4096]{2,1,0:T(8,128)} %bitcast.13, s32[3,1,4096]{2,1,0:T(1,128)} %broadcast_in_dim.6.length_ref, bf16[32,64,128]{2,1,0:T(8,128)(2,1)} %narrow_dpool.1.refs_0_), custom_call_target="tpu_custom_call" | custom-call | flops 10000000 | bytes 1024 | tf_op jit(solution)/shard_map/count_hits/pallas_call | solution.py:261
  62.7 5.5 %wide_sum.1.wide_ref = f32[512,256]{1,0:T(8,128)} custom-call(s32[3,64,4096]{2,1,0:T(8,128)} %count_hits.1.hits_ref, bf16[4096,128]{1,0:T(8,128)(2,1)} %bitcast.11, bf16[256,128]{1,0:T(8,128)(2,1)} %bitcast.15), custom_call_target="tpu_custom_call" | custom-call | flops 10000000 | bytes 1024 | tf_op jit(solution)/shard_map/wide_sum/pallas_call | solution.py:299
  68.2 0.9 %collective-permute-done.11 = bf16[4,256,128]{2,1,0:T(8,128)(2,1)S(1)} collective-permute-done((bf16[4,256,128]{2,1,0:T(8,128)(2,1)S(1)}, bf16[4,256,128]{2,1,0:T(8,128)(2,1)S(1)}, u32[]{:S(2)}, u32[]{:S(2)}) %collective-permute-start.11) | collective-permute-done | bytes 262176 | tf_op jit(solution)/shard_map/ppermute | solution.py:362
  69.2 4.6 %collective-permute-done.10 = bf16[4,256,128]{2,1,0:T(8,128)(2,1)S(1)} collective-permute-done((bf16[4,256,128]{2,1,0:T(8,128)(2,1)S(1)}, bf16[4,256,128]{2,1,0:T(8,128)(2,1)S(1)}, u32[]{:S(2)}, u32[]{:S(2)}) %collective-permute-start.10) | collective-permute-done | bytes 262176 | tf_op jit(solution)/shard_map/ppermute | solution.py:362
  74.0 1.8 %collective-permute-start.12 = (bf16[1,256,128]{2,1,0:T(8,128)(2,1)S(1)}, bf16[1,256,128]{2,1,0:T(8,128)(2,1)S(1)}, u32[]{:S(2)}, u32[]{:S(2)}) collective-permute-start(bf16[1,256,128]{2,1,0:T(8,128)(2,1)S(1)} %get-tuple-element.52), channel_id=1, source_target_pairs={{0,1},{1,0},{2,3},{3,2},{4,5},{5,4},{6,7},{7,6},{8,9},{9,8},{10,11... | collective-permute-start | bytes 196616 | tf_op jit(solution)/shard_map/ppermute | solution.py:362
  75.8 1.9 %collective-permute-start.13 = (bf16[1,256,128]{2,1,0:T(8,128)(2,1)S(1)}, bf16[1,256,128]{2,1,0:T(8,128)(2,1)S(1)}, u32[]{:S(2)}, u32[]{:S(2)}) collective-permute-start(bf16[1,256,128]{2,1,0:T(8,128)(2,1)S(1)} %get-tuple-element.51), channel_id=1, source_target_pairs={{0,2},{1,3},{2,0},{3,1},{4,6},{5,7},{6,4},{7,5},{8,10},{9,11},{10,... | collective-permute-start | bytes 196616 | tf_op jit(solution)/shard_map/ppermute | solution.py:362
  77.6 0.8 collective-permute-start.14
  78.4 0.8 copy-done.1
  79.2 5.4 %narrow_sum.1 = f32[512,256]{1,0:T(8,128)} custom-call(s32[3,64,4096]{2,1,0:T(8,128)} %count_hits.1.hits_ref, bf16[32,64,128]{2,1,0:T(8,128)(2,1)} %copy-done.1, f32[512,256]{1,0:T(8,128)} %wide_sum.1.wide_ref), custom_call_target="tpu_custom_call", output_to_operand_aliasing={{}: (2, {})} | custom-call | flops 10000000 | bytes 1024 | tf_op jit(solution)/shard_map/narrow_sum/pallas_call | solution.py:343
  (54 shorter events, 6.8 us)
Async XLA Ops:
  1.4 12.1 %collective-permute-start.2 = (bf16[1,64,128]{2,1,0:T(8,128)(2,1)S(1)}, bf16[1,64,128]{2,1,0:T(8,128)(2,1)S(1)}, u32[]{:S(2)}, u32[]{:S(2)}) collective-permute-start(bf16[1,64,128]{2,1,0:T(8,128)(2,1)S(1)} %slice.15), channel_id=1, source_target_pairs={{0,3},{1,2},{2,1},{3,0},{4,7},{5,6},{6,5},{7,4},{8,11},{9,10},{10,... | collective-permute-start | bytes 49160 | tf_op jit(solution)/shard_map/ppermute | solution.py:362
  6.4 7.1 %collective-permute-start.1 = (bf16[1,64,128]{2,1,0:T(8,128)(2,1)S(1)}, bf16[1,64,128]{2,1,0:T(8,128)(2,1)S(1)}, u32[]{:S(2)}, u32[]{:S(2)}) collective-permute-start(bf16[1,64,128]{2,1,0:T(8,128)(2,1)S(1)} %slice.15), channel_id=1, source_target_pairs={{0,2},{1,3},{2,0},{3,1},{4,6},{5,7},{6,4},{7,5},{8,10},{9,11},{10,... | collective-permute-start | bytes 49160 | tf_op jit(solution)/shard_map/ppermute | solution.py:362
  6.4 7.1 %collective-permute-start = (bf16[1,64,128]{2,1,0:T(8,128)(2,1)S(1)}, bf16[1,64,128]{2,1,0:T(8,128)(2,1)S(1)}, u32[]{:S(2)}, u32[]{:S(2)}) collective-permute-start(bf16[1,64,128]{2,1,0:T(8,128)(2,1)S(1)} %slice.15), channel_id=1, source_target_pairs={{0,1},{1,0},{2,3},{3,2},{4,5},{5,4},{6,7},{7,6},{8,9},{9,8},{10,11... | collective-permute-start | bytes 49160 | tf_op jit(solution)/shard_map/ppermute | solution.py:362
  13.5 34.2 %all-to-all-start = ((bf16[32,128,128]{2,1,0:T(8,128)(2,1)}), bf16[32,128,128]{2,1,0:T(8,128)(2,1)S(1)}, u32[]{:S(2)}, u32[]{:S(2)}) async-start(bf16[32,128,128]{2,1,0:T(8,128)(2,1)} %get-tuple-element.30.refs_2_), calls=%async_computation | async-start | bytes 2097152 | tf_op jit(solution)/shard_map/all_to_all | solution.py:376
  24.5 12.2 %collective-permute-start.7 = (f32[8,256,128]{2,1,0:T(8,128)}, f32[8,256,128]{2,1,0:T(8,128)S(1)}, u32[]{:S(2)}, u32[]{:S(2)}) collective-permute-start(f32[8,256,128]{2,1,0:T(8,128)} %get-tuple-element.31), channel_id=1, source_target_pairs={{0,4},{4,0},{8,12},{12,8},{16,20},{20,16},{24,28},{28,24},{1,5},{5... | collective-permute-start | bytes 3145736 | tf_op jit(solution)/shard_map/ppermute | solution.py:362
  24.8 11.9 %collective-permute-start.8 = (f32[8,256,128]{2,1,0:T(8,128)}, f32[8,256,128]{2,1,0:T(8,128)S(1)}, u32[]{:S(2)}, u32[]{:S(2)}) collective-permute-start(f32[8,256,128]{2,1,0:T(8,128)} %get-tuple-element.32), channel_id=1, source_target_pairs={{0,4},{4,0},{8,12},{12,8},{16,20},{20,16},{24,28},{28,24},{1,5},{5... | collective-permute-start | bytes 3145736 | tf_op jit(solution)/shard_map/ppermute | solution.py:362
  26.2 5.2 %collective-permute-start.3 = (bf16[4,64,128]{2,1,0:T(8,128)(2,1)S(1)}, bf16[4,64,128]{2,1,0:T(8,128)(2,1)S(1)}, u32[]{:S(2)}, u32[]{:S(2)}) collective-permute-start(bf16[4,64,128]{2,1,0:T(8,128)(2,1)S(1)} %pad_maximum_fusion.1), channel_id=1, source_target_pairs={{0,8},{4,12},{8,0},{12,4},{16,24},{20,28},{24,16},{28,20},{1,9},{5... | collective-permute-start | bytes 196616 | tf_op jit(solution)/shard_map/ppermute | solution.py:362
  27.9 6.7 %collective-permute-start.4 = (bf16[4,64,128]{2,1,0:T(8,128)(2,1)S(1)}, bf16[4,64,128]{2,1,0:T(8,128)(2,1)S(1)}, u32[]{:S(2)}, u32[]{:S(2)}) collective-permute-start(bf16[4,64,128]{2,1,0:T(8,128)(2,1)S(1)} %pad_maximum_fusion.1), channel_id=1, source_target_pairs={{0,16},{4,20},{8,24},{12,28},{16,0},{20,4},{24,8},{28,12},{1,17},{... | collective-permute-start | bytes 196616 | tf_op jit(solution)/shard_map/ppermute | solution.py:362
  29.4 5.7 %collective-permute-start.5 = (bf16[4,64,128]{2,1,0:T(8,128)(2,1)S(1)}, bf16[4,64,128]{2,1,0:T(8,128)(2,1)S(1)}, u32[]{:S(2)}, u32[]{:S(2)}) collective-permute-start(bf16[4,64,128]{2,1,0:T(8,128)(2,1)S(1)} %pad_maximum_fusion.1), channel_id=1, source_target_pairs={{0,24},{4,28},{8,16},{12,20},{16,8},{20,12},{24,0},{28,4},{1,25},{... | collective-permute-start | bytes 196616 | tf_op jit(solution)/shard_map/ppermute | solution.py:362
  35.1 1.6 %collective-permute-start.6 = (bf16[16,64,128]{2,1,0:T(8,128)(2,1)S(1)}, bf16[16,64,128]{2,1,0:T(8,128)(2,1)S(1)}, u32[]{:S(2)}, u32[]{:S(2)}) collective-permute-start(bf16[16,64,128]{2,1,0:T(8,128)(2,1)S(1)} %pad_maximum_fusion), channel_id=1, source_target_pairs={{0,4},{4,0},{8,12},{12,8},{16,20},{20,16},{24,28},{28,24},{1,5},{5... | collective-permute-start | bytes 786440 | tf_op jit(solution)/shard_map/ppermute | solution.py:362
  36.8 6.5 %copy-start.5 = (bf16[32,64,128]{2,1,0:T(8,128)(2,1)}, bf16[32,64,128]{2,1,0:T(8,128)(2,1)S(1)}, u32[]{:S(2)}) copy-start(bf16[32,64,128]{2,1,0:T(8,128)(2,1)S(1)} %constant_dynamic-update-slice_fusion.w_ref) | copy-start | bytes 1572868
  43.2 10.3 %copy-start.9 = (bf16[4,256,128]{2,1,0:T(8,128)(2,1)S(1)}, bf16[4,256,128]{2,1,0:T(8,128)(2,1)}, u32[]{:S(2)}) copy-start(bf16[4,256,128]{2,1,0:T(8,128)(2,1)} %get-tuple-element.41) | copy-start | bytes 786436
  43.2 13.1 %copy-start.8 = (bf16[4,256,128]{2,1,0:T(8,128)(2,1)S(1)}, bf16[4,256,128]{2,1,0:T(8,128)(2,1)}, u32[]{:S(2)}) copy-start(bf16[4,256,128]{2,1,0:T(8,128)(2,1)} %get-tuple-element.40) | copy-start | bytes 786436
  43.2 13.6 %copy-start.7 = (bf16[4,256,128]{2,1,0:T(8,128)(2,1)S(1)}, bf16[4,256,128]{2,1,0:T(8,128)(2,1)}, u32[]{:S(2)}) copy-start(bf16[4,256,128]{2,1,0:T(8,128)(2,1)} %get-tuple-element.39) | copy-start | bytes 786436
  43.2 13.9 %copy-start.6 = (s32[1,4096,3]{1,0,2:T(1,128)S(1)}, s32[1,4096,3]{1,0,2:T(1,128)}, u32[]{:S(2)}) copy-start(s32[1,4096,3]{1,0,2:T(1,128)} %param.11) | copy-start | bytes 147460
  47.8 15.0 %copy-start = (bf16[32,128,128]{2,1,0:T(8,128)(2,1)}, bf16[32,128,128]{2,1,0:T(8,128)(2,1)S(1)}, u32[]{:S(2)}) copy-start(bf16[32,128,128]{2,1,0:T(8,128)(2,1)S(1)} %all-to-all-done) | copy-start | bytes 3145732
  47.8 30.7 %all-to-all-start.1 = ((bf16[32,64,128]{2,1,0:T(8,128)(2,1)}), bf16[32,64,128]{2,1,0:T(8,128)(2,1)S(1)}, u32[]{:S(2)}, u32[]{:S(2)}) async-start(bf16[32,64,128]{2,1,0:T(8,128)(2,1)} %narrow_dpool.1.refs_0_), calls=%async_computation.1 | async-start | bytes 1048576 | tf_op jit(solution)/shard_map/all_to_all | solution.py:395
  53.5 15.6 %collective-permute-start.11 = (bf16[4,256,128]{2,1,0:T(8,128)(2,1)S(1)}, bf16[4,256,128]{2,1,0:T(8,128)(2,1)S(1)}, u32[]{:S(2)}, u32[]{:S(2)}) collective-permute-start(bf16[4,256,128]{2,1,0:T(8,128)(2,1)S(1)} %copy-done.9), channel_id=1, source_target_pairs={{0,24},{4,28},{8,16},{12,20},{16,8},{20,12},{24,0},{28,4},{1,25},{... | collective-permute-start | bytes 786440 | tf_op jit(solution)/shard_map/ppermute | solution.py:362
  56.3 17.5 %collective-permute-start.10 = (bf16[4,256,128]{2,1,0:T(8,128)(2,1)S(1)}, bf16[4,256,128]{2,1,0:T(8,128)(2,1)S(1)}, u32[]{:S(2)}, u32[]{:S(2)}) collective-permute-start(bf16[4,256,128]{2,1,0:T(8,128)(2,1)S(1)} %copy-done.8), channel_id=1, source_target_pairs={{0,16},{4,20},{8,24},{12,28},{16,0},{20,4},{24,8},{28,12},{1,17},{... | collective-permute-start | bytes 786440 | tf_op jit(solution)/shard_map/ppermute | solution.py:362
  56.8 17.0 %collective-permute-start.9 = (bf16[4,256,128]{2,1,0:T(8,128)(2,1)S(1)}, bf16[4,256,128]{2,1,0:T(8,128)(2,1)S(1)}, u32[]{:S(2)}, u32[]{:S(2)}) collective-permute-start(bf16[4,256,128]{2,1,0:T(8,128)(2,1)S(1)} %copy-done.7), channel_id=1, source_target_pairs={{0,8},{4,12},{8,0},{12,4},{16,24},{20,28},{24,16},{28,20},{1,9},{5... | collective-permute-start | bytes 786440 | tf_op jit(solution)/shard_map/ppermute | solution.py:362
  62.7 11.1 %copy-start.2 = (f32[4,256,128]{2,1,0:T(8,128)S(1)}, f32[4,256,128]{2,1,0:T(8,128)}, u32[]{:S(2)}) copy-start(f32[4,256,128]{2,1,0:T(8,128)} %get-tuple-element.38.refs_0_) | copy-start | bytes 1572868
  74.0 10.6 %collective-permute-start.12 = (bf16[1,256,128]{2,1,0:T(8,128)(2,1)S(1)}, bf16[1,256,128]{2,1,0:T(8,128)(2,1)S(1)}, u32[]{:S(2)}, u32[]{:S(2)}) collective-permute-start(bf16[1,256,128]{2,1,0:T(8,128)(2,1)S(1)} %get-tuple-element.52), channel_id=1, source_target_pairs={{0,1},{1,0},{2,3},{3,2},{4,5},{5,4},{6,7},{7,6},{8,9},{9,8},{10,11... | collective-permute-start | bytes 196616 | tf_op jit(solution)/shard_map/ppermute | solution.py:362
  75.8 8.9 %collective-permute-start.13 = (bf16[1,256,128]{2,1,0:T(8,128)(2,1)S(1)}, bf16[1,256,128]{2,1,0:T(8,128)(2,1)S(1)}, u32[]{:S(2)}, u32[]{:S(2)}) collective-permute-start(bf16[1,256,128]{2,1,0:T(8,128)(2,1)S(1)} %get-tuple-element.51), channel_id=1, source_target_pairs={{0,2},{1,3},{2,0},{3,1},{4,6},{5,7},{6,4},{7,5},{8,10},{9,11},{10,... | collective-permute-start | bytes 196616 | tf_op jit(solution)/shard_map/ppermute | solution.py:362
  77.6 7.0 %collective-permute-start.14 = (bf16[1,256,128]{2,1,0:T(8,128)(2,1)S(1)}, bf16[1,256,128]{2,1,0:T(8,128)(2,1)S(1)}, u32[]{:S(2)}, u32[]{:S(2)}) collective-permute-start(bf16[1,256,128]{2,1,0:T(8,128)(2,1)S(1)} %get-tuple-element.50), channel_id=1, source_target_pairs={{0,3},{1,2},{2,1},{3,0},{4,7},{5,6},{6,5},{7,4},{8,11},{9,10},{10,... | collective-permute-start | bytes 196616 | tf_op jit(solution)/shard_map/ppermute | solution.py:362
  (3 other events, 2.8 us)

commit v3 on v2

--- a/solution.py
+++ b/solution.py
@@ -154,7 +154,7 @@
             ],
         ),
         compiler_params=params(1),
-        cost_estimate=cost(1e7),
+        cost_estimate=cost(4e9),
         name="narrow_dpool",
     )(place, g12, w12, *after)
 
@@ -228,7 +228,7 @@
             ],
         ),
         compiler_params=params(1),
-        cost_estimate=cost(1e7),
+        cost_estimate=cost(4e9 if others else 1e7),
         name="partial_proj",
     )(nodes, lines, *operands, *others)
 
@@ -269,7 +269,7 @@
         + [ANY] * len(after),
         out_specs=pl.BlockSpec((1, ROWS // 8, block), lambda k, i: (k, 0, i)),
         compiler_params=params(2),
-        cost_estimate=cost(1e7),
+        cost_estimate=cost(5e9),
         name="count_hits",
     )(lookups, counts, *after)
 
@@ -382,19 +382,20 @@
 
     rows, sent = lax.optimization_barrier((rows, sent))
     rows = jnp.concatenate([rows] + [swap(rows, "node", n_node, 2 * d) for d in range(1, n_plane)])
+    hits = count_hits(indices[0].transpose(1, 2, 0), lengths[0].T[:, None, :], after=sent[:1])
     kept = partial_proj(plane * 2 + node % 2, lines, q, g12, g3, n_plane, got)
+    farthest = swap(kept[-1], "node", n_node, 2 * (n_plane - 1))
 
     rows = jnp.concatenate([rows, swap(rows, "node", n_node, 1)])
     slot = jnp.arange(slots, dtype=jnp.int32)
     slot_node = slot // n_local ^ node
     slot_place = slot_node % 2 * (slots // 2) + slot_node // 2 * n_local + (slot % n_local ^ loc)
     narrow = narrow_dpool(slot_place, g12, rows, after=kept[:1])
-    hits = count_hits(indices[0].transpose(1, 2, 0), lengths[0].T[:, None, :], after=[narrow])
-
-    narrow, g3_got, kept = lax.optimization_barrier((narrow, g3_got, kept))
+
+    narrow, hits, g3_got, kept, farthest = lax.optimization_barrier((narrow, hits, g3_got, kept, farthest))
     narrow_got = lax.all_to_all(narrow, AXES, split_axis=0, concat_axis=0, tiled=True)
-    total = kept[0]
-    for d in range(1, n_plane):
+    total = kept[0] + farthest.astype(jnp.float32)
+    for d in range(1, n_plane - 1):
         total = total + swap(kept[d], "node", n_node, 2 * d).astype(jnp.float32)
     wide = wide_sum(hits, g3_got.reshape(-1, PD), proj[0])
     total, wide = lax.optimization_barrier((total, wide))

time: 86 us -> 84.9 us (0.987)
  waiting for transfers between devices: 12.5 us -> 9.06 us
  starting transfers between devices: 29.6 us -> 31.8 us
    ppermute x15, waiting for transfers between devices: 12.5 us -> 9.06 us  [swap(): return lax.ppermute(x, axis, [(d, d ^ bits) for d in range(size)])]
    ppermute x15, starting transfers between devices: 17.8 us -> 20.2 us  [swap(): return lax.ppermute(x, axis, [(d, d ^ bits) for d in range(size)])]
    unnamed x25 -> x23, local copies, waits for them, and re-layouts: 2.88 us -> 2.96 us
  transfers between devices with their start and end apart: 17 -> 17, of which waited for: 6 -> 3; matrix products, arithmetic and copies ran while one was open for 3% -> 3% of each run, Pallas kernels for 42% -> 42%
where the time goes in v3:
time: 84.9 us; the launch traced here: 84.2 us
  Pallas kernels  35.5 us (42%)
  starting transfers between devices  31.8 us (37%)
  waiting for transfers between devices  9.06 us (11%)
  local copies, waits for them, and re-layouts  4.39 us (5%)
  other arithmetic  2.52 us (3%)
  between operations  0.88 us (1%)
    ppermute x15, starting transfers between devices, swap(): return lax.ppermute(x, axis, [(d, d ^ bits) for d in range(size)])  20.2 us
    ppermute x15, waiting for transfers between devices, swap(): return lax.ppermute(x, axis, [(d, d ^ bits) for d in range(size)])  9.06 us
    pallas_call x2, Pallas kernels, partial_proj(): pl.pallas_call(functools.partial(partial_kernel, len(operands), len(other...  8.76 us
    pallas_call x1, Pallas kernels, permute(): pl.pallas_call(functools.partial(permute_kernel, slots, pieces), out_shap...  6.5 us
    all_to_all x1, starting transfers between devices, local(): g3_got = lax.all_to_all(g3, AXES, split_axis=0, concat_axis=0, tiled=True)  6.07 us
    all_to_all x1, starting transfers between devices, local(): lax.all_to_all(narrow, AXES, split_axis=0, concat_axis=0, tiled=True)  5.52 us
    pallas_call x1, Pallas kernels, wide_sum(): pl.pallas_call(wide_kernel, out_shape=jax.ShapeDtypeStruct((ROWS, WSUM),...  5.47 us
    pallas_call x1, Pallas kernels, narrow_sum(): pl.pallas_call(narrow_sum_kernel, out_shape=jax.ShapeDtypeStruct((ROWS, W...  5.39 us
  transfers between devices with their start and end apart: 17, of which 3 were waited for; matrix products, arithmetic and copies ran while one was open for 3% of the time, Pallas kernels for 42%

profile of v3, /device:TPU:0, one launch (start us, length us, event | category | flops | bytes accessed | tf_op | source)
XLA Modules:
  0.0 84.2 jit_solution(3265976347427407202)
XLA Ops:
  0.6 0.7 slice.15
  1.4 5.0 %collective-permute-start.2 = (bf16[1,64,128]{2,1,0:T(8,128)(2,1)S(1)}, bf16[1,64,128]{2,1,0:T(8,128)(2,1)S(1)}, u32[]{:S(2)}, u32[]{:S(2)}) collective-permute-start(bf16[1,64,128]{2,1,0:T(8,128)(2,1)S(1)} %slice.15), channel_id=1, source_target_pairs={{0,3},{1,2},{2,1},{3,0},{4,7},{5,6},{6,5},{7,4},{8,11},{9,10},{10,... | collective-permute-start | bytes 49160 | tf_op jit(solution)/shard_map/ppermute | solution.py:362
  7.6 6.5 %permute_groups.1 = (bf16[32,128,256]{2,1,0:T(8,128)(2,1)}, bf16[32,128,128]{2,1,0:T(8,128)(2,1)}, bf16[32,128,256]{2,1,0:T(8,128)(2,1)}) custom-call(s32[32]{0:T(128)} %assign_ref.1, bf16[128,32,384]{2,1,0:T(8,128)(2,1)} %grad_ref.1, bf16[128,32,256]{2,1,0:T(8,128)(2,1)} %pool_ref.1), custom_call_target="tpu_custom_call" | custom-call | flops 10000000 | bytes 1024 | tf_op jit(solution)/shard_map/permute_groups/pallas_call | solution.py:78
  14.1 6.1 %all-to-all-start = ((bf16[32,128,128]{2,1,0:T(8,128)(2,1)}), bf16[32,128,128]{2,1,0:T(8,128)(2,1)S(1)}, u32[]{:S(2)}, u32[]{:S(2)}) async-start(bf16[32,128,128]{2,1,0:T(8,128)(2,1)} %get-tuple-element.32.refs_2_), calls=%async_computation | async-start | bytes 2097152 | tf_op jit(solution)/shard_map/all_to_all | solution.py:376
  22.0 4.3 %partial_proj.2 = (f32[8,256,128]{2,1,0:T(8,128)}, f32[8,256,128]{2,1,0:T(8,128)}) custom-call(s32[4]{0:T(128)} %get-tuple-element.58.node_ref, s32[4]{0:T(128)} %get-tuple-element.57.line_ref, bf16[32,128,256]{2,1,0:T(8,128)(2,1)} %get-tuple-element.31.refs_0_, bf16[32,128,256]{2,1,0:T(8,128)(2,1)} %get-tuple-element.28.refs_1_.g_ref, ...), custom_call_target="tpu_custom_call" | custom-call | flops 10000000 | bytes 1024 | tf_op jit(solution)/shard_map/partial_proj/pallas_call | solution.py:213
  26.3 1.8 %collective-permute-start.3 = (bf16[4,64,128]{2,1,0:T(8,128)(2,1)S(1)}, bf16[4,64,128]{2,1,0:T(8,128)(2,1)S(1)}, u32[]{:S(2)}, u32[]{:S(2)}) collective-permute-start(bf16[4,64,128]{2,1,0:T(8,128)(2,1)S(1)} %pad_maximum_fusion.1), channel_id=1, source_target_pairs={{0,8},{4,12},{8,0},{12,4},{16,24},{20,28},{24,16},{28,20},{1,9},{5... | collective-permute-start | bytes 196616 | tf_op jit(solution)/shard_map/ppermute | solution.py:362
  28.1 1.5 %collective-permute-start.4 = (bf16[4,64,128]{2,1,0:T(8,128)(2,1)S(1)}, bf16[4,64,128]{2,1,0:T(8,128)(2,1)S(1)}, u32[]{:S(2)}, u32[]{:S(2)}) collective-permute-start(bf16[4,64,128]{2,1,0:T(8,128)(2,1)S(1)} %pad_maximum_fusion.1), channel_id=1, source_target_pairs={{0,16},{4,20},{8,24},{12,28},{16,0},{20,4},{24,8},{28,12},{1,17},{... | collective-permute-start | bytes 196616 | tf_op jit(solution)/shard_map/ppermute | solution.py:362
  30.4 4.9 %count_hits.1.hits_ref = s32[3,64,4096]{2,1,0:T(8,128)} custom-call(s32[3,8,4096]{2,1,0:T(8,128)} %bitcast.15, s32[3,1,4096]{2,1,0:T(1,128)} %broadcast_in_dim.6.length_ref, f32[8,256,128]{2,1,0:T(8,128)} %get-tuple-element.37.refs_0_), custom_call_target="tpu_custom_call" | custom-call | flops 5000000000 | bytes 1024 | tf_op jit(solution)/shard_map/count_hits/pallas_call | solution.py:261
  35.5 1.5 %collective-permute-done.6 = bf16[16,64,128]{2,1,0:T(8,128)(2,1)S(1)} collective-permute-done((bf16[16,64,128]{2,1,0:T(8,128)(2,1)S(1)}, bf16[16,64,128]{2,1,0:T(8,128)(2,1)S(1)}, u32[]{:S(2)}, u32[]{:S(2)}) %collective-permute-start.6) | collective-permute-done | bytes 262176 | tf_op jit(solution)/shard_map/ppermute | solution.py:362
  37.1 1.0 %copy-done.5 = f32[8,256,128]{2,1,0:T(8,128)} copy-done((f32[8,256,128]{2,1,0:T(8,128)}, f32[8,256,128]{2,1,0:T(8,128)S(1)}, u32[]{:S(2)}) %copy-start.5) | copy-done | bytes 1048600
  38.1 1.0 %copy-done.6 = f32[8,256,128]{2,1,0:T(8,128)} copy-done((f32[8,256,128]{2,1,0:T(8,128)}, f32[8,256,128]{2,1,0:T(8,128)S(1)}, u32[]{:S(2)}) %copy-start.6) | copy-done | bytes 1048600
  39.1 4.4 %partial_proj.3 = (f32[4,256,128]{2,1,0:T(8,128)}, bf16[4,256,128]{2,1,0:T(8,128)(2,1)}, bf16[4,256,128]{2,1,0:T(8,128)(2,1)}, bf16[4,256,128]{2,1,0:T(8,128)(2,1)}) custom-call(s32[4]{0:T(128)} %fusion.5.node_ref, s32[4]{0:T(128)} %get-tuple-element.57.line_ref, bf16[32,128,256]{2,1,0:T(8,128)(2,1)} %get-tuple-element.31.refs_0_, ...), custom_call_target="tpu_custom_call" | custom-call | flops 4000000000 | bytes 1024 | tf_op jit(solution)/shard_map/partial_proj/pallas_call | solution.py:213
  43.6 2.7 %collective-permute-start.9 = (bf16[4,256,128]{2,1,0:T(8,128)(2,1)}, bf16[4,256,128]{2,1,0:T(8,128)(2,1)S(1)}, u32[]{:S(2)}, u32[]{:S(2)}) collective-permute-start(bf16[4,256,128]{2,1,0:T(8,128)(2,1)} %get-tuple-element.40), channel_id=1, source_target_pairs={{0,24},{4,28},{8,16},{12,20},{16,8},{20,12},{24,0},{28,4},{1,25},{... | collective-permute-start | bytes 786440 | tf_op jit(solution)/shard_map/ppermute | solution.py:362
  46.3 4.5 %narrow_dpool.1 = bf16[32,64,128]{2,1,0:T(8,128)(2,1)} custom-call(s32[32]{0:T(128)} %fusion.1.place_ref, bf16[32,128,256]{2,1,0:T(8,128)(2,1)} %get-tuple-element.28.refs_1_.g_ref, bf16[32,64,128]{2,1,0:T(8,128)(2,1)} %copy-done.4, f32[4,256,128]{2,1,0:T(8,128)} %get-tuple-element.41.refs_0_), custom_call_target="tpu_custom_call" | custom-call | flops 4000000000 | bytes 1024 | tf_op jit(solution)/shard_map/narrow_dpool/pallas_call | solution.py:139
  50.8 2.6 %collective-permute-done.9 = bf16[4,256,128]{2,1,0:T(8,128)(2,1)S(1)} collective-permute-done((bf16[4,256,128]{2,1,0:T(8,128)(2,1)}, bf16[4,256,128]{2,1,0:T(8,128)(2,1)S(1)}, u32[]{:S(2)}, u32[]{:S(2)}) %collective-permute-start.9) | collective-permute-done | bytes 262176 | tf_op jit(solution)/shard_map/ppermute | solution.py:362
  53.4 5.5 %all-to-all-start.1 = ((bf16[32,64,128]{2,1,0:T(8,128)(2,1)}), bf16[32,64,128]{2,1,0:T(8,128)(2,1)S(1)}, u32[]{:S(2)}, u32[]{:S(2)}) async-start(bf16[32,64,128]{2,1,0:T(8,128)(2,1)} %narrow_dpool.1), calls=%async_computation.1 | async-start | bytes 1048576 | tf_op jit(solution)/shard_map/all_to_all | solution.py:396
  58.9 1.8 %collective-permute-start.11 = (bf16[4,256,128]{2,1,0:T(8,128)(2,1)S(1)}, bf16[4,256,128]{2,1,0:T(8,128)(2,1)S(1)}, u32[]{:S(2)}, u32[]{:S(2)}) collective-permute-start(bf16[4,256,128]{2,1,0:T(8,128)(2,1)S(1)} %copy-done.8), channel_id=1, source_target_pairs={{0,16},{4,20},{8,24},{12,28},{16,0},{20,4},{24,8},{28,12},{1,17},{... | collective-permute-start | bytes 786440 | tf_op jit(solution)/shard_map/ppermute | solution.py:362
  60.8 1.5 %collective-permute-start.10 = (bf16[4,256,128]{2,1,0:T(8,128)(2,1)S(1)}, bf16[4,256,128]{2,1,0:T(8,128)(2,1)S(1)}, u32[]{:S(2)}, u32[]{:S(2)}) collective-permute-start(bf16[4,256,128]{2,1,0:T(8,128)(2,1)S(1)} %copy-done.7), channel_id=1, source_target_pairs={{0,8},{4,12},{8,0},{12,4},{16,24},{20,28},{24,16},{28,20},{1,9},{5... | collective-permute-start | bytes 786440 | tf_op jit(solution)/shard_map/ppermute | solution.py:362
  62.2 5.5 %wide_sum.1.wide_ref = f32[512,256]{1,0:T(8,128)} custom-call(s32[3,64,4096]{2,1,0:T(8,128)} %count_hits.1.hits_ref, bf16[4096,128]{1,0:T(8,128)(2,1)} %bitcast.11, bf16[256,128]{1,0:T(8,128)(2,1)} %bitcast.14), custom_call_target="tpu_custom_call" | custom-call | flops 10000000 | bytes 1024 | tf_op jit(solution)/shard_map/wide_sum/pallas_call | solution.py:299
  67.7 5.0 %collective-permute-done.11 = bf16[4,256,128]{2,1,0:T(8,128)(2,1)S(1)} collective-permute-done((bf16[4,256,128]{2,1,0:T(8,128)(2,1)S(1)}, bf16[4,256,128]{2,1,0:T(8,128)(2,1)S(1)}, u32[]{:S(2)}, u32[]{:S(2)}) %collective-permute-start.11) | collective-permute-done | bytes 262176 | tf_op jit(solution)/shard_map/ppermute | solution.py:362
  72.9 1.7 %collective-permute-start.12 = (bf16[1,256,128]{2,1,0:T(8,128)(2,1)S(1)}, bf16[1,256,128]{2,1,0:T(8,128)(2,1)S(1)}, u32[]{:S(2)}, u32[]{:S(2)}) collective-permute-start(bf16[1,256,128]{2,1,0:T(8,128)(2,1)S(1)} %get-tuple-element.56), channel_id=1, source_target_pairs={{0,1},{1,0},{2,3},{3,2},{4,5},{5,4},{6,7},{7,6},{8,9},{9,8},{10,11... | collective-permute-start | bytes 196616 | tf_op jit(solution)/shard_map/ppermute | solution.py:362
  74.6 2.6 %collective-permute-start.13 = (bf16[1,256,128]{2,1,0:T(8,128)(2,1)S(1)}, bf16[1,256,128]{2,1,0:T(8,128)(2,1)S(1)}, u32[]{:S(2)}, u32[]{:S(2)}) collective-permute-start(bf16[1,256,128]{2,1,0:T(8,128)(2,1)S(1)} %get-tuple-element.55), channel_id=1, source_target_pairs={{0,2},{1,3},{2,0},{3,1},{4,6},{5,7},{6,4},{7,5},{8,10},{9,11},{10,... | collective-permute-start | bytes 196616 | tf_op jit(solution)/shard_map/ppermute | solution.py:362
  77.3 0.8 copy-done.1
  78.1 5.4 %narrow_sum.1 = f32[512,256]{1,0:T(8,128)} custom-call(s32[3,64,4096]{2,1,0:T(8,128)} %count_hits.1.hits_ref, bf16[32,64,128]{2,1,0:T(8,128)(2,1)} %copy-done.1, f32[512,256]{1,0:T(8,128)} %wide_sum.1.wide_ref), custom_call_target="tpu_custom_call", output_to_operand_aliasing={{}: (2, {})} | custom-call | flops 10000000 | bytes 1024 | tf_op jit(solution)/shard_map/narrow_sum/pallas_call | solution.py:343
  (52 shorter events, 4.9 us)
Async XLA Ops:
  1.4 12.7 %collective-permute-start.2 = (bf16[1,64,128]{2,1,0:T(8,128)(2,1)S(1)}, bf16[1,64,128]{2,1,0:T(8,128)(2,1)S(1)}, u32[]{:S(2)}, u32[]{:S(2)}) collective-permute-start(bf16[1,64,128]{2,1,0:T(8,128)(2,1)S(1)} %slice.15), channel_id=1, source_target_pairs={{0,3},{1,2},{2,1},{3,0},{4,7},{5,6},{6,5},{7,4},{8,11},{9,10},{10,... | collective-permute-start | bytes 49160 | tf_op jit(solution)/shard_map/ppermute | solution.py:362
  6.4 7.7 %collective-permute-start.1 = (bf16[1,64,128]{2,1,0:T(8,128)(2,1)S(1)}, bf16[1,64,128]{2,1,0:T(8,128)(2,1)S(1)}, u32[]{:S(2)}, u32[]{:S(2)}) collective-permute-start(bf16[1,64,128]{2,1,0:T(8,128)(2,1)S(1)} %slice.15), channel_id=1, source_target_pairs={{0,2},{1,3},{2,0},{3,1},{4,6},{5,7},{6,4},{7,5},{8,10},{9,11},{10,... | collective-permute-start | bytes 49160 | tf_op jit(solution)/shard_map/ppermute | solution.py:362
  6.4 7.7 %collective-permute-start = (bf16[1,64,128]{2,1,0:T(8,128)(2,1)S(1)}, bf16[1,64,128]{2,1,0:T(8,128)(2,1)S(1)}, u32[]{:S(2)}, u32[]{:S(2)}) collective-permute-start(bf16[1,64,128]{2,1,0:T(8,128)(2,1)S(1)} %slice.15), channel_id=1, source_target_pairs={{0,1},{1,0},{2,3},{3,2},{4,5},{5,4},{6,7},{7,6},{8,9},{9,8},{10,11... | collective-permute-start | bytes 49160 | tf_op jit(solution)/shard_map/ppermute | solution.py:362
  14.1 6.7 %copy-start.3 = (s32[1,4096,3]{1,0,2:T(1,128)S(1)}, s32[1,4096,3]{1,0,2:T(1,128)}, u32[]{:S(2)}) copy-start(s32[1,4096,3]{1,0,2:T(1,128)} %param.11) | copy-start | bytes 147460
  14.1 39.3 %all-to-all-start = ((bf16[32,128,128]{2,1,0:T(8,128)(2,1)}), bf16[32,128,128]{2,1,0:T(8,128)(2,1)S(1)}, u32[]{:S(2)}, u32[]{:S(2)}) async-start(bf16[32,128,128]{2,1,0:T(8,128)(2,1)} %get-tuple-element.32.refs_2_), calls=%async_computation | async-start | bytes 2097152 | tf_op jit(solution)/shard_map/all_to_all | solution.py:376
  26.3 9.0 %collective-permute-start.3 = (bf16[4,64,128]{2,1,0:T(8,128)(2,1)S(1)}, bf16[4,64,128]{2,1,0:T(8,128)(2,1)S(1)}, u32[]{:S(2)}, u32[]{:S(2)}) collective-permute-start(bf16[4,64,128]{2,1,0:T(8,128)(2,1)S(1)} %pad_maximum_fusion.1), channel_id=1, source_target_pairs={{0,8},{4,12},{8,0},{12,4},{16,24},{20,28},{24,16},{28,20},{1,9},{5... | collective-permute-start | bytes 196616 | tf_op jit(solution)/shard_map/ppermute | solution.py:362
  28.1 7.2 %collective-permute-start.4 = (bf16[4,64,128]{2,1,0:T(8,128)(2,1)S(1)}, bf16[4,64,128]{2,1,0:T(8,128)(2,1)S(1)}, u32[]{:S(2)}, u32[]{:S(2)}) collective-permute-start(bf16[4,64,128]{2,1,0:T(8,128)(2,1)S(1)} %pad_maximum_fusion.1), channel_id=1, source_target_pairs={{0,16},{4,20},{8,24},{12,28},{16,0},{20,4},{24,8},{28,12},{1,17},{... | collective-permute-start | bytes 196616 | tf_op jit(solution)/shard_map/ppermute | solution.py:362
  29.6 5.7 %collective-permute-start.5 = (bf16[4,64,128]{2,1,0:T(8,128)(2,1)S(1)}, bf16[4,64,128]{2,1,0:T(8,128)(2,1)S(1)}, u32[]{:S(2)}, u32[]{:S(2)}) collective-permute-start(bf16[4,64,128]{2,1,0:T(8,128)(2,1)S(1)} %pad_maximum_fusion.1), channel_id=1, source_target_pairs={{0,24},{4,28},{8,16},{12,20},{16,8},{20,12},{24,0},{28,4},{1,25},{... | collective-permute-start | bytes 196616 | tf_op jit(solution)/shard_map/ppermute | solution.py:362
  29.9 7.2 %collective-permute-start.7 = (f32[8,256,128]{2,1,0:T(8,128)}, f32[8,256,128]{2,1,0:T(8,128)S(1)}, u32[]{:S(2)}, u32[]{:S(2)}) collective-permute-start(f32[8,256,128]{2,1,0:T(8,128)} %get-tuple-element.37.refs_0_), channel_id=1, source_target_pairs={{0,4},{4,0},{8,12},{12,8},{16,20},{20,16},{24,28},{28,24},{1,5},{5... | collective-permute-start | bytes 3145736 | tf_op jit(solution)/shard_map/ppermute | solution.py:362
  29.9 7.2 %collective-permute-start.8 = (f32[8,256,128]{2,1,0:T(8,128)}, f32[8,256,128]{2,1,0:T(8,128)S(1)}, u32[]{:S(2)}, u32[]{:S(2)}) collective-permute-start(f32[8,256,128]{2,1,0:T(8,128)} %get-tuple-element.34), channel_id=1, source_target_pairs={{0,4},{4,0},{8,12},{12,8},{16,20},{20,16},{24,28},{28,24},{1,5},{5... | collective-permute-start | bytes 3145736 | tf_op jit(solution)/shard_map/ppermute | solution.py:362
  35.4 1.6 %collective-permute-start.6 = (bf16[16,64,128]{2,1,0:T(8,128)(2,1)S(1)}, bf16[16,64,128]{2,1,0:T(8,128)(2,1)S(1)}, u32[]{:S(2)}, u32[]{:S(2)}) collective-permute-start(bf16[16,64,128]{2,1,0:T(8,128)(2,1)S(1)} %pad_maximum_fusion), channel_id=1, source_target_pairs={{0,4},{4,0},{8,12},{12,8},{16,20},{20,16},{24,28},{28,24},{1,5},{5... | collective-permute-start | bytes 786440 | tf_op jit(solution)/shard_map/ppermute | solution.py:362
  37.0 6.5 %copy-start.4 = (bf16[32,64,128]{2,1,0:T(8,128)(2,1)}, bf16[32,64,128]{2,1,0:T(8,128)(2,1)S(1)}, u32[]{:S(2)}) copy-start(bf16[32,64,128]{2,1,0:T(8,128)(2,1)S(1)} %constant_dynamic-update-slice_fusion.w_ref) | copy-start | bytes 1572868
  37.1 1.1 %copy-start.5 = (f32[8,256,128]{2,1,0:T(8,128)}, f32[8,256,128]{2,1,0:T(8,128)S(1)}, u32[]{:S(2)}) copy-start(f32[8,256,128]{2,1,0:T(8,128)S(1)} %collective-permute-done.7.refs_3_) | copy-start | bytes 3145732
  43.6 9.8 %collective-permute-start.9 = (bf16[4,256,128]{2,1,0:T(8,128)(2,1)}, bf16[4,256,128]{2,1,0:T(8,128)(2,1)S(1)}, u32[]{:S(2)}, u32[]{:S(2)}) collective-permute-start(bf16[4,256,128]{2,1,0:T(8,128)(2,1)} %get-tuple-element.40), channel_id=1, source_target_pairs={{0,24},{4,28},{8,16},{12,20},{16,8},{20,12},{24,0},{28,4},{1,25},{... | collective-permute-start | bytes 786440 | tf_op jit(solution)/shard_map/ppermute | solution.py:362
  46.3 12.6 %copy-start.8 = (bf16[4,256,128]{2,1,0:T(8,128)(2,1)S(1)}, bf16[4,256,128]{2,1,0:T(8,128)(2,1)}, u32[]{:S(2)}) copy-start(bf16[4,256,128]{2,1,0:T(8,128)(2,1)} %get-tuple-element.44) | copy-start | bytes 786436
  46.3 14.5 %copy-start.7 = (bf16[4,256,128]{2,1,0:T(8,128)(2,1)S(1)}, bf16[4,256,128]{2,1,0:T(8,128)(2,1)}, u32[]{:S(2)}) copy-start(bf16[4,256,128]{2,1,0:T(8,128)(2,1)} %get-tuple-element.43) | copy-start | bytes 786436
  53.4 8.8 %copy-start = (bf16[32,128,128]{2,1,0:T(8,128)(2,1)}, bf16[32,128,128]{2,1,0:T(8,128)(2,1)S(1)}, u32[]{:S(2)}) copy-start(bf16[32,128,128]{2,1,0:T(8,128)(2,1)S(1)} %all-to-all-done) | copy-start | bytes 3145732
  53.4 23.9 %all-to-all-start.1 = ((bf16[32,64,128]{2,1,0:T(8,128)(2,1)}), bf16[32,64,128]{2,1,0:T(8,128)(2,1)S(1)}, u32[]{:S(2)}, u32[]{:S(2)}) async-start(bf16[32,64,128]{2,1,0:T(8,128)(2,1)} %narrow_dpool.1), calls=%async_computation.1 | async-start | bytes 1048576 | tf_op jit(solution)/shard_map/all_to_all | solution.py:396
  58.9 13.7 %collective-permute-start.11 = (bf16[4,256,128]{2,1,0:T(8,128)(2,1)S(1)}, bf16[4,256,128]{2,1,0:T(8,128)(2,1)S(1)}, u32[]{:S(2)}, u32[]{:S(2)}) collective-permute-start(bf16[4,256,128]{2,1,0:T(8,128)(2,1)S(1)} %copy-done.8), channel_id=1, source_target_pairs={{0,16},{4,20},{8,24},{12,28},{16,0},{20,4},{24,8},{28,12},{1,17},{... | collective-permute-start | bytes 786440 | tf_op jit(solution)/shard_map/ppermute | solution.py:362
  60.8 11.9 %collective-permute-start.10 = (bf16[4,256,128]{2,1,0:T(8,128)(2,1)S(1)}, bf16[4,256,128]{2,1,0:T(8,128)(2,1)S(1)}, u32[]{:S(2)}, u32[]{:S(2)}) collective-permute-start(bf16[4,256,128]{2,1,0:T(8,128)(2,1)S(1)} %copy-done.7), channel_id=1, source_target_pairs={{0,8},{4,12},{8,0},{12,4},{16,24},{20,28},{24,16},{28,20},{1,9},{5... | collective-permute-start | bytes 786440 | tf_op jit(solution)/shard_map/ppermute | solution.py:362
  62.2 10.4 %copy-start.2 = (f32[4,256,128]{2,1,0:T(8,128)S(1)}, f32[4,256,128]{2,1,0:T(8,128)}, u32[]{:S(2)}) copy-start(f32[4,256,128]{2,1,0:T(8,128)} %get-tuple-element.41.refs_0_) | copy-start | bytes 1572868
  72.9 10.7 %collective-permute-start.12 = (bf16[1,256,128]{2,1,0:T(8,128)(2,1)S(1)}, bf16[1,256,128]{2,1,0:T(8,128)(2,1)S(1)}, u32[]{:S(2)}, u32[]{:S(2)}) collective-permute-start(bf16[1,256,128]{2,1,0:T(8,128)(2,1)S(1)} %get-tuple-element.56), channel_id=1, source_target_pairs={{0,1},{1,0},{2,3},{3,2},{4,5},{5,4},{6,7},{7,6},{8,9},{9,8},{10,11... | collective-permute-start | bytes 196616 | tf_op jit(solution)/shard_map/ppermute | solution.py:362
  74.6 9.0 %collective-permute-start.13 = (bf16[1,256,128]{2,1,0:T(8,128)(2,1)S(1)}, bf16[1,256,128]{2,1,0:T(8,128)(2,1)S(1)}, u32[]{:S(2)}, u32[]{:S(2)}) collective-permute-start(bf16[1,256,128]{2,1,0:T(8,128)(2,1)S(1)} %get-tuple-element.55), channel_id=1, source_target_pairs={{0,2},{1,3},{2,0},{3,1},{4,6},{5,7},{6,4},{7,5},{8,10},{9,11},{10,... | collective-permute-start | bytes 196616 | tf_op jit(solution)/shard_map/ppermute | solution.py:362
  77.2 6.3 %collective-permute-start.14 = (bf16[1,256,128]{2,1,0:T(8,128)(2,1)S(1)}, bf16[1,256,128]{2,1,0:T(8,128)(2,1)S(1)}, u32[]{:S(2)}, u32[]{:S(2)}) collective-permute-start(bf16[1,256,128]{2,1,0:T(8,128)(2,1)S(1)} %get-tuple-element.54), channel_id=1, source_target_pairs={{0,3},{1,2},{2,1},{3,0},{4,7},{5,6},{6,5},{7,4},{8,11},{9,10},{10,... | collective-permute-start | bytes 196616 | tf_op jit(solution)/shard_map/ppermute | solution.py:362
  (2 other events, 1.8 us)
